TPU v7x, 32 devices: a whole 2x2x4 slice. The times are simulated.
32 devices in a mesh: groups: 2 (over x), row: 8 (over z, y), col: 2 (over core).
Axes of the slice: x: 2, y: 2, z: 4, core: 2. Of those that a mesh axis runs over, the one named last changes fastest.
Arguments:
- prefix_states: bfloat16 [2048, 8192], P(('groups', 'col'), 'row'), parts along dimension 0, may hold values from -480 to 480
- prefix_gain: float32 [8192], P('row'), may hold values from 0.1 to 1.9
- backbone_key: bfloat16 [8192, 1024], P('row', 'col'), may hold values from -0.0625 to 0.0625
- backbone_value: bfloat16 [8192, 1024], P('row', 'col'), may hold values from -0.0625 to 0.0625
- action_states: bfloat16 [16384, 2048], P(('groups', 'row'), 'col'), parts along dimension 0, may hold values from -14 to 14
- expert_query: bfloat16 [2048, 2048], P('row', 'col'), may hold values from -0.25 to 0.25
- expert_key: bfloat16 [2048, 1024], P('row', 'col'), may hold values from -0.125 to 0.125
- expert_value: bfloat16 [2048, 1024], P('row', 'col'), may hold values from -0.125 to 0.125
- expert_out: bfloat16 [2048, 2048], P('col', 'row'), may hold values from -0.5 to 0.5
- prefix_length: int32 [16], P(('groups', 'row')), parts along dimension 0, may hold values from 32 to 128, as said below
- action_length: int32 [16], P(('groups', 'row')), parts along dimension 0, may hold values from 256 to 1024, as said below
Outputs:
- prefix_keys: bfloat16 [2048, 1024], P(('groups', 'row'), 'col'), parts along dimension 0
- prefix_values: bfloat16 [2048, 1024], P(('groups', 'row'), 'col'), parts along dimension 0
- action_out: bfloat16 [16384, 2048], P(('groups', 'row'), 'col'), parts along dimension 0
There are 2 independent parts, one for each index of `groups`. A program takes and returns all parts, laid end to end along the dimension named above; an argument that names none is the same for every part. Nothing has to cross between parts.
Inputs may be any that keep to these rules, and one draw needn't show every extreme that they name: `prefix_length`: every draw has an episode with all 128 prefix tokens valid. `action_length`: every draw has an episode with all 1024 action tokens valid.
All inputs are finite; a program needn't handle non-finite values.
Results may differ from a plain program's by a relative error of at most 0.0095.
Values may be sent and summed in bfloat16 or wider, within the bound.
A program may use at most 128 MiB of HBM per device.

v0:
```python
import jax
import jax.numpy as jnp
from jax import lax
from jax.sharding import PartitionSpec as P

D = 8192
HEAD = 128


def shards(
    prefix_states,
    prefix_gain,
    backbone_key,
    backbone_value,
    action_states,
    expert_query,
    expert_key,
    expert_value,
    expert_out,
    prefix_length,
    action_length,
):
    states = prefix_states.astype(jnp.float32)
    squares = lax.psum(jnp.sum(states * states, axis=1), "row")
    normed = (states * lax.rsqrt(squares[:, None] / D + 1e-06) * prefix_gain[None, :]).astype(
        jnp.bfloat16
    )
    all_rows = lax.all_gather(normed, "col", axis=0, tiled=True)
    key_cols = backbone_key.shape[1]
    joined = jnp.concatenate([backbone_key, backbone_value], axis=1)
    summed = lax.psum_scatter(
        jnp.dot(all_rows, joined, preferred_element_type=jnp.float32),
        "row",
        scatter_dimension=0,
        tiled=True,
    )
    key_sum = summed[:, :key_cols]
    value_sum = summed[:, key_cols:]
    prefix_keys = key_sum.astype(jnp.bfloat16)
    prefix_values = value_sum.astype(jnp.bfloat16)
    action_rows = lax.all_gather(action_states, "col", axis=1, tiled=True)
    token_count = action_rows.shape[0]
    query_cols = expert_query.shape[1]
    value_cols = expert_key.shape[1]
    pieces = (
        lax.all_gather(expert_query, "row", axis=0, tiled=True),
        lax.all_gather(expert_key, "row", axis=0, tiled=True),
        lax.all_gather(expert_value, "row", axis=0, tiled=True),
    )
    query_total, key_total, value_total = tuple(
        (
            jnp.dot(action_rows, weight_piece, preferred_element_type=jnp.float32)
            for weight_piece in pieces
        )
    )
    action_query = query_total.astype(jnp.bfloat16)
    action_key = key_total.astype(jnp.bfloat16)
    action_value = value_total.astype(jnp.bfloat16)
    local_groups = value_cols // HEAD
    prefix_count = prefix_keys.shape[0]
    keys_all = jnp.concatenate([prefix_keys, action_key], axis=0).reshape(
        prefix_count + token_count, local_groups, HEAD
    )
    values_all = jnp.concatenate([prefix_values, action_value], axis=0).reshape(
        prefix_count + token_count, local_groups, HEAD
    )
    valid = jnp.concatenate(
        [jnp.arange(prefix_count) < prefix_length[0], jnp.arange(token_count) < action_length[0]]
    )
    block_size = min(512, token_count)
    query_blocks = action_query.reshape(
        token_count // block_size, block_size, local_groups, 2, HEAD
    )
    scale_factor = HEAD ** (-0.5)

    def attend_block(query_block):
        scores = (
            jnp.einsum("qgjd,kgd->gjqk", query_block, keys_all, preferred_element_type=jnp.float32)
            * scale_factor
        )
        scores = jnp.where(valid[None, None, None, :], scores, -1e30)
        highest = jnp.max(scores, axis=-1, keepdims=True)
        exponent = jnp.exp(scores - highest)
        weights = (exponent / jnp.sum(exponent, axis=-1, keepdims=True)).astype(jnp.bfloat16)
        return jnp.einsum(
            "gjqk,kgd->qgjd", weights, values_all, preferred_element_type=jnp.float32
        ).astype(jnp.bfloat16)

    attended = lax.map(attend_block, query_blocks).reshape(token_count, query_cols)
    terms = jnp.dot(
        attended,
        lax.all_gather(expert_out, "row", axis=1, tiled=True),
        preferred_element_type=jnp.float32,
    )
    action_out = lax.psum_scatter(terms, "col", scatter_dimension=1, tiled=True).astype(
        jnp.bfloat16
    )
    return (prefix_keys, prefix_values, action_out)


def solution(mesh):
    placed = (
        P(("groups", "col"), "row"),
        P("row"),
        P("row", "col"),
        P("row", "col"),
        P(("groups", "row"), "col"),
        P("row", "col"),
        P("row", "col"),
        P("row", "col"),
        P("col", "row"),
        P(("groups", "row")),
        P(("groups", "row")),
    )
    return jax.shard_map(
        shards,
        mesh=mesh,
        in_specs=placed,
        out_specs=(
            P(("groups", "row"), "col"),
            P(("groups", "row"), "col"),
            P(("groups", "row"), "col"),
        ),
        check_vma=False,
    )
```

profile of v0, /device:TPU:0, one launch (start us, length us, event | category | flops | bytes accessed | tf_op | source)
XLA Modules:
  0.0 436.5 jit_solution(9103008433536940796)
XLA Ops:
  8.7 23.1 %psum.7 = f32[512]{0:T(512)S(1)} all-reduce(f32[512]{0:T(512)S(1)} %fusion.28), channel_id=1, replica_groups=mesh['groups'=2,'row'=8,'col'=2] {'row'}, use_global_device_ids=true, to_apply=%region_1.0 | all-reduce | flops 512 | bytes 4096 | tf_op jit(solution)/shard_map/psum | solution.py:24
  31.8 2.5 fusion.30
  37.1 5.3 %all-gather.7.cloned.1.call-done = bf16[1024,1024]{1,0:T(8,128)(2,1)} async-done(((bf16[512,1024]{1,0:T(8,128)(2,1)}), bf16[1024,1024]{1,0:T(8,128)(2,1)}) %all-gather.7.cloned.1.call-update) | async-done | bytes 2097168 | tf_op jit(solution)/shard_map/all_gather | solution.py:28
  42.4 5.9 %fusion.31 = f32[1024,1024]{1,0:T(8,128)} fusion(bf16[1024,1024]{1,0:T(8,128)(2,1)} %all-gather.7.cloned.1.call-done, bf16[1024,512]{1,0:T(8,128)(2,1)S(1)} %copy-done.2, bf16[1024,512]{1,0:T(8,128)(2,1)S(1)} %copy-done.3), kind=kOutput, calls=%fused_computation.27 | convolution fusion | flops 2151677952 | bytes 8388608 | tf_op jit(solution)/shard_map/dot_general | solution.py:32
  50.4 44.6 %all-gather.13.cloned.1.call-done = bf16[2048,512]{1,0:T(8,128)(2,1)} async-done(((bf16[256,512]{1,0:T(8,128)(2,1)}), bf16[2048,512]{1,0:T(8,128)(2,1)}) %all-gather.13.cloned.1.call-update) | async-done | bytes 2097168 | tf_op jit(solution)/shard_map/all_gather | solution.py:47
  95.0 13.7 %all-gather.9.cloned.1.call-done = bf16[1024,2048]{1,0:T(8,128)(2,1)} async-done(((bf16[1024,1024]{1,0:T(8,128)(2,1)}), bf16[1024,2048]{1,0:T(8,128)(2,1)}) %all-gather.9.cloned.1.call-update) | async-done | bytes 4194320 | tf_op jit(solution)/shard_map/all_gather | solution.py:41
  108.7 5.2 %convolution_convert_fusion.2 = bf16[1024,512]{1,0:T(8,128)(2,1)S(1)} fusion(bf16[1024,2048]{1,0:T(8,128)(2,1)} %all-gather.9.cloned.1.call-done, bf16[2048,512]{1,0:T(8,128)(2,1)} %all-gather.13.cloned.1.call-done), kind=kOutput, calls=%fused_computation.33 | convolution fusion | flops 2148007936 | bytes 7340032 | tf_op jit(solution)/shard_map/dot_general | solution.py:52
  113.9 47.3 %all-gather.15.cloned.1.call-done = bf16[2048,512]{1,0:T(8,128)(2,1)} async-done(((bf16[256,512]{1,0:T(8,128)(2,1)}), bf16[2048,512]{1,0:T(8,128)(2,1)}) %all-gather.15.cloned.1.call-update) | async-done | bytes 2097168 | tf_op jit(solution)/shard_map/all_gather | solution.py:48
  161.2 6.2 %convolution_convert_fusion.1 = bf16[1024,512]{1,0:T(8,128)(2,1)} fusion(bf16[1024,2048]{1,0:T(8,128)(2,1)} %all-gather.9.cloned.1.call-done, bf16[2048,512]{1,0:T(8,128)(2,1)} %all-gather.15.cloned.1.call-done), kind=kOutput, calls=%fused_computation.32 | convolution fusion | flops 2148007936 | bytes 7340032 | tf_op jit(solution)/shard_map/dot_general | solution.py:52
  167.4 67.7 %all-gather.11.cloned.1.call-done = bf16[2048,1024]{1,0:T(8,128)(2,1)} async-done(((bf16[256,1024]{1,0:T(8,128)(2,1)}), bf16[2048,1024]{1,0:T(8,128)(2,1)}) %all-gather.11.cloned.1.call-update) | async-done | bytes 4194320 | tf_op jit(solution)/shard_map/all_gather | solution.py:46
  235.1 7.9 %convolution_convert_fusion = bf16[1024,1024]{1,0:T(8,128)(2,1)S(1)} fusion(bf16[1024,2048]{1,0:T(8,128)(2,1)} %all-gather.9.cloned.1.call-done, bf16[2048,1024]{1,0:T(8,128)(2,1)} %all-gather.11.cloned.1.call-done), kind=kOutput, calls=%fused_computation.31 | convolution fusion | flops 4296015872 | bytes 10485760 | tf_op jit(solution)/shard_map/dot_general | solution.py:52
  243.1 2.7 reshape.26
  245.8 79.0 %reduce-scatter.3.cloned.1.call-done = f32[128,1024]{1,0:T(8,128)} async-done(((f32[1024,1024]{1,0:T(8,128)}), f32[128,1024]{1,0:T(8,128)}) %reduce-scatter.3.cloned.1.call-update) | async-done | bytes 524304 | tf_op jit(solution)/shard_map/reduce_scatter | solution.py:31
  325.9 2.8 copy_bitcast_fusion.7
  328.7 42.4 %while.10 = (s32[]{:T(128)}, bf16[2,512,4,2,128]{4,3,2,1,0:T(2,128)(2,1)}, pred[1152]{0:T(1024)(128)(4,1)S(1)}, bf16[2,512,4,2,128]{4,3,2,1,0:T(2,128)(2,1)}, bf...) while((s32[]{:T(128)}, bf16[2,512,4,2,128]{4,3,2,1,0:T(2,128)(2,1)}, ...), condition=%wide.region_6.7_spmd, body=%wide.region_3.6_spmd.sunk | while | flops 3666876416 | bytes 10914141 | solution.py:89
  330.6 7.4 %exponential_reduce_fusion.2 = f32[4,2,512]{2,1,0:T(2,128)S(1)} fusion(pred[1152]{0:T(1024)(128)(4,1)S(1)} %get-tuple-element.117, bf16[1152,4,128]{2,0,1:T(8,128)(2,1)} %get-tuple-element.119, bf16[1,512,4,2,128]{4,3,2,1,0:T(2,128)(2,1)S(1)} %constant_dynamic-slice_fusion.2), kind=kOutput, calls=%fused_computation.7.clone.1 | convolution fusion | flops 1226835072 | bytes 2245760 | tf_op jit(solution)/shard_map/while/body/eval_jaxpr/sub | solution.py:83
  338.0 9.8 %fusion.58 = bf16[1,512,4,2,128]{4,1,3,2,0:T(8,128)(2,1)S(1)} fusion(f32[4,2,512]{2,1,0:T(2,128)S(1)} %exponential_reduce_fusion.2, bf16[1152,4,128]{2,0,1:T(8,128)(2,1)S(1)} %get-tuple-element.120, pred[1152]{0:T(1024)(128)(4,1)S(1)} %get-tuple-element.117, bf16[1152,4,128]{2,0,1:T(8,128)(2,1)} %get-tuple-element.119, ...), kind=kOutput, calls=%fused_computation.10.clone.1 | convolution fusion | flops 2440041472 | bytes 4473984 | tf_op jit(solution)/shard_map/while/body/eval_jaxpr/gjqk,kgd->qgjd/dot_general | solution.py:85
  351.8 7.4 %exponential_reduce_fusion.2 = f32[4,2,512]{2,1,0:T(2,128)S(1)} fusion(pred[1152]{0:T(1024)(128)(4,1)S(1)} %get-tuple-element.117, bf16[1152,4,128]{2,0,1:T(8,128)(2,1)} %get-tuple-element.119, bf16[1,512,4,2,128]{4,3,2,1,0:T(2,128)(2,1)S(1)} %constant_dynamic-slice_fusion.2), kind=kOutput, calls=%fused_computation.7.clone.1 | convolution fusion | flops 1226835072 | bytes 2245760 | tf_op jit(solution)/shard_map/while/body/eval_jaxpr/sub | solution.py:83
  359.2 9.8 %fusion.58 = bf16[1,512,4,2,128]{4,1,3,2,0:T(8,128)(2,1)S(1)} fusion(f32[4,2,512]{2,1,0:T(2,128)S(1)} %exponential_reduce_fusion.2, bf16[1152,4,128]{2,0,1:T(8,128)(2,1)S(1)} %get-tuple-element.120, pred[1152]{0:T(1024)(128)(4,1)S(1)} %get-tuple-element.117, bf16[1152,4,128]{2,0,1:T(8,128)(2,1)} %get-tuple-element.119, ...), kind=kOutput, calls=%fused_computation.10.clone.1 | convolution fusion | flops 2440041472 | bytes 4473984 | tf_op jit(solution)/shard_map/while/body/eval_jaxpr/gjqk,kgd->qgjd/dot_general | solution.py:85
  371.1 3.2 reshape.29
  374.3 27.5 %all-gather.17.cloned.1.call-done = bf16[1024,2048]{1,0:T(8,128)(2,1)} async-done(((bf16[1024,256]{1,0:T(8,128)(2,1)}), bf16[1024,2048]{1,0:T(8,128)(2,1)}) %all-gather.17.cloned.1.call-update) | async-done | bytes 4194320 | tf_op jit(solution)/shard_map/all_gather | solution.py:92
  401.8 8.8 %fusion.39 = f32[1024,2048]{1,0:T(8,128)} fusion(bf16[1024,1024]{1,0:T(8,128)(2,1)S(1)} %reshape.29, bf16[1024,2048]{1,0:T(8,128)(2,1)} %all-gather.17.cloned.1.call-done), kind=kOutput, calls=%fused_computation.44 | convolution fusion | flops 4294967296 | bytes 14680064 | tf_op jit(solution)/shard_map/dot_general | solution.py:90
  410.7 15.1 %reduce-scatter.5.cloned.1.call-done = f32[1024,1024]{1,0:T(8,128)} async-done(((f32[1024,2048]{1,0:T(8,128)}), f32[1024,1024]{1,0:T(8,128)}) %reduce-scatter.5.cloned.1.call-update) | async-done | bytes 4194320 | tf_op jit(solution)/shard_map/reduce_scatter | solution.py:95
  425.8 3.8 convert_element_type.34
  (36 shorter events, 14.1 us)
Async XLA Ops:
  7.2 35.2 %all-gather.7.cloned.1.call-start = ((), (), s32[]{:S(2)}) async-start(), calls=%async_computation.2 | async-start | bytes 3145728 | tf_op jit(solution)/shard_map/all_gather | solution.py:28
  34.4 8.0 %copy-start.2 = (bf16[1024,512]{1,0:T(8,128)(2,1)S(1)}, bf16[1024,512]{1,0:T(8,128)(2,1)}, u32[]{:S(2)}) copy-start(bf16[1024,512]{1,0:T(8,128)(2,1)} %param.16) | copy-start | bytes 3145732
  34.4 8.0 %copy-start.3 = (bf16[1024,512]{1,0:T(8,128)(2,1)S(1)}, bf16[1024,512]{1,0:T(8,128)(2,1)}, u32[]{:S(2)}) copy-start(bf16[1024,512]{1,0:T(8,128)(2,1)} %param.15) | copy-start | bytes 3145732
  34.4 60.6 %all-gather.13.cloned.1.call-start = ((), (), s32[]{:S(2)}) async-start(), calls=%async_computation.6 | async-start | bytes 2359296 | tf_op jit(solution)/shard_map/all_gather | solution.py:47
  35.1 73.6 %all-gather.9.cloned.1.call-start = ((), (), s32[]{:S(2)}) async-start(), calls=%async_computation.4 | async-start | bytes 6291456 | tf_op jit(solution)/shard_map/all_gather | solution.py:41
  35.9 125.3 %all-gather.15.cloned.1.call-start = ((), (), s32[]{:S(2)}) async-start(), calls=%async_computation.7 | async-start | bytes 2359296 | tf_op jit(solution)/shard_map/all_gather | solution.py:48
  36.4 198.7 %all-gather.11.cloned.1.call-start = ((), (), s32[]{:S(2)}) async-start(), calls=%async_computation.5 | async-start | bytes 4718592 | tf_op jit(solution)/shard_map/all_gather | solution.py:46
  37.0 287.7 %reduce-scatter.3.cloned.1.call-start = ((), (), s32[]{:S(2)}) async-start(), calls=%async_computation.3 | async-start | bytes 4718592 | tf_op jit(solution)/shard_map/reduce_scatter | solution.py:31
  48.3 353.5 %all-gather.17.cloned.1.call-start = ((), (), s32[]{:S(2)}) async-start(), calls=%async_computation.8 | async-start | bytes 4718592 | tf_op jit(solution)/shard_map/all_gather | solution.py:92
  49.0 376.8 %reduce-scatter.5.cloned.1.call-start = ((), (), s32[]{:S(2)}) async-start(), calls=%async_computation.9 | async-start | bytes 12582912 | tf_op jit(solution)/shard_map/reduce_scatter | solution.py:95
  325.9 2.8 copy-start
  325.9 2.8 copy-start.1
Sparse Core Ops, SparseCore 0:
  34.5 7.8 all-gather.6
  44.5 50.4 all-gather.12
  96.5 12.1 all-gather.8
  110.7 50.4 all-gather.14
  163.2 71.8 all-gather.10
  238.6 86.1 reduce-scatter.2
  327.0 74.7 all-gather.16
  410.8 14.9 reduce-scatter.4
where the time goes:
time: 437 us
  waiting for transfers between devices  303 us (69%)
  matrix products  68.4 us (16%)
  blocking collectives  23.1 us (5%)
  between operations  15.5 us (4%)
  local copies, waits for them, and re-layouts  14 us (3%)
  other arithmetic  11.7 us (3%)
    reduce_scatter x1, waiting for transfers between devices, shards(): lax.psum_scatter(jnp.dot(all_rows, joined, preferred_element_type=jnp.flo...  79 us
    all_gather x1, waiting for transfers between devices, shards(): lax.all_gather(expert_query, 'row', axis=0, tiled=True)  67.7 us
    all_gather x1, waiting for transfers between devices, shards(): lax.all_gather(expert_value, 'row', axis=0, tiled=True)  47.3 us
    all_gather x1, waiting for transfers between devices, shards(): lax.all_gather(expert_key, 'row', axis=0, tiled=True)  44.6 us
    all_gather x1, waiting for transfers between devices, shards(): lax.all_gather(expert_out, 'row', axis=1, tiled=True)  27.5 us
    psum x1, blocking collectives, shards(): squares = lax.psum(jnp.sum(states * states, axis=1), 'row')  23.1 us
    dot_general x2, matrix products, attend_block(): jnp.einsum('gjqk,kgd->qgjd', weights, values_all, preferred_element_type=...  19.6 us
    dot_general x3, matrix products, shards(): jnp.dot(action_rows, weight_piece, preferred_element_type=jnp.float32)  19.3 us
  transfers between devices with their start and end apart: 8, of which 8 were waited for; matrix products, arithmetic and copies ran while one was open for 18% of the time, Pallas kernels for 0%

commit v1 on v0

v1 whole, which is shorter than its diff:
```python
import functools
import math

import jax
import jax.numpy as jnp
import numpy as np
from jax import lax
from jax.experimental import pallas as pl
from jax.experimental.pallas import tpu as pltpu
from jax.sharding import PartitionSpec as P

HEAD = 128
F32 = jnp.float32
BF16 = jnp.bfloat16


def attend_kernel(scale, plen_ref, alen_ref, q_ref, pk_ref, ak_ref, pv_ref, av_ref, o_ref):
    nt = (((1,), (1,)), ((), ()))
    prefix_count, token_count = pk_ref.shape[0], ak_ref.shape[0]
    prefix_bias = jnp.where(
        lax.broadcasted_iota(jnp.int32, (1, prefix_count), 1) < plen_ref[0], 0.0, -1e30
    )
    action_bias = jnp.where(
        lax.broadcasted_iota(jnp.int32, (1, token_count), 1) < alen_ref[0], 0.0, -1e30
    )
    for j in range(q_ref.shape[1] // HEAD):
        cols = slice(j * HEAD, (j + 1) * HEAD)
        q = q_ref[:, cols]
        sp = lax.dot_general(q, pk_ref[...], nt, preferred_element_type=F32) + prefix_bias
        sa = lax.dot_general(q, ak_ref[...], nt, preferred_element_type=F32) + action_bias
        top = jnp.maximum(
            jnp.max(sp, axis=-1, keepdims=True), jnp.max(sa, axis=-1, keepdims=True)
        )
        ep = jnp.exp2((sp - top) * scale)
        ea = jnp.exp2((sa - top) * scale)
        total = jnp.sum(ep, axis=-1, keepdims=True) + jnp.sum(ea, axis=-1, keepdims=True)
        out = jnp.dot(ep.astype(BF16), pv_ref[...], preferred_element_type=F32)
        out += jnp.dot(ea.astype(BF16), av_ref[...], preferred_element_type=F32)
        o_ref[:, cols] = (out / total).astype(BF16)


def attend(plen, alen, query, pk, ak, pv, av):
    tokens, query_cols = query.shape
    groups = ak.shape[1] // HEAD
    width = query_cols // groups
    rows = math.gcd(tokens, 256)
    keys = pk.shape[0] + ak.shape[0]
    smem = pl.BlockSpec(memory_space=pltpu.SMEM)
    return pl.pallas_call(
        functools.partial(attend_kernel, HEAD**-0.5 * math.log2(math.e)),
        grid=(groups, tokens // rows),
        in_specs=[
            smem,
            smem,
            pl.BlockSpec((rows, width), lambda g, i: (i, g)),
            pl.BlockSpec((pk.shape[0], HEAD), lambda g, i: (0, g)),
            pl.BlockSpec((ak.shape[0], HEAD), lambda g, i: (0, g)),
            pl.BlockSpec((pv.shape[0], HEAD), lambda g, i: (0, g)),
            pl.BlockSpec((av.shape[0], HEAD), lambda g, i: (0, g)),
        ],
        out_specs=pl.BlockSpec((rows, width), lambda g, i: (i, g)),
        out_shape=jax.ShapeDtypeStruct((tokens, query_cols), BF16),
        compiler_params=pltpu.CompilerParams(vmem_limit_bytes=32 * 1024 * 1024),
        cost_estimate=pl.CostEstimate(
            flops=8 * tokens * query_cols * keys,
            bytes_accessed=4 * tokens * query_cols,
            transcendentals=tokens * keys * query_cols // HEAD,
        ),
        name="attend",
    )(plen, alen, query, pk, ak, pv, av)


def shards(
    mesh,
    prefix_states,
    prefix_gain,
    backbone_key,
    backbone_value,
    action_states,
    expert_query,
    expert_key,
    expert_value,
    expert_out,
    prefix_length,
    action_length,
):
    count = mesh.shape["row"]
    ring = list(range(0, count, 2)) + list(range(count - 1, 0, -2))
    place = np.argsort(np.array(ring))
    shifts = np.array(
        [[ring[(place[r] + s) % count] for s in range(count)] for r in range(count)], np.uint32
    )
    ahead = [(ring[p], ring[(p + 1) % count]) for p in range(count)]
    back = [(b, a) for a, b in ahead]
    mine = lax.axis_index("row").astype(jnp.uint32)
    zero = jnp.uint32(0)
    shifted = lax.dynamic_slice(jnp.array(shifts), (mine, zero), (1, count))
    col = lax.axis_index("col").astype(jnp.uint32)
    swap = [(0, 1), (1, 0)]

    def row_at(shift):
        return shifted[0, shift % count]

    def cut(array, start, size, axis):
        begin = (start, zero) if axis == 0 else (zero, start)
        sizes = (size, array.shape[1]) if axis == 0 else (array.shape[0], size)
        return lax.dynamic_slice(array, begin, sizes)

    def gather(block):
        got = []
        ahead_block = back_block = block
        for step in range(1, count // 2):
            ahead_block = lax.ppermute(ahead_block, "row", ahead)
            back_block = lax.ppermute(back_block, "row", back)
            got.append((row_at(-step), ahead_block, row_at(step), back_block))
        half = block.shape[0] // 2
        last = jnp.concatenate(
            [
                lax.ppermute(ahead_block[:half], "row", ahead),
                lax.ppermute(back_block[half:], "row", back),
            ],
            axis=0,
        )
        return got, (row_at(count // 2), last)

    def both(block, axis):
        other = lax.ppermute(block, "col", swap)
        low = jnp.where(col == 0, block, other)
        high = jnp.where(col == 0, other, block)
        return jnp.concatenate([low, high], axis=axis)

    joined = jnp.concatenate([expert_query, expert_key, expert_value], axis=1)
    weight_pairs, weight_last = gather(joined)

    states = both(prefix_states, 0)
    wide = states.astype(F32)
    squares = jnp.sum(wide * wide, axis=1)
    features = prefix_states.shape[1] * count
    all_squares = lax.all_gather(squares, "row", axis=0)
    scaled = (wide * prefix_gain[None, :]).astype(BF16)
    key_part = jnp.dot(scaled, backbone_key, preferred_element_type=F32)
    value_part = jnp.dot(scaled, backbone_value, preferred_element_type=F32)
    own = states.shape[0] // count

    def part(array, row):
        return cut(array, row * own, own, 0)

    key_run = part(key_part, row_at(-1))
    value_run = part(value_part, row_at(1))
    for step in range(count - 1):
        key_run = lax.ppermute(key_run.astype(BF16), "row", ahead).astype(F32)
        value_run = lax.ppermute(value_run.astype(BF16), "row", back).astype(F32)
        key_run += part(key_part, row_at(-2 - step))
        value_run += part(value_part, row_at(2 + step - count))
    own_squares = lax.dynamic_slice(jnp.sum(all_squares, axis=0), (mine * own,), (own,))
    row_scale = lax.rsqrt(own_squares / features + 1e-06)[:, None]
    prefix_keys = (key_run * row_scale).astype(BF16)
    prefix_values = (value_run * row_scale).astype(BF16)

    actions = both(action_states, 1)
    depth = joined.shape[0]

    def columns(row):
        return cut(actions, row * depth, depth, 1)

    total = jnp.dot(columns(mine), joined, preferred_element_type=F32)
    for row_a, block_a, row_b, block_b in weight_pairs:
        total += jnp.dot(
            jnp.concatenate([columns(row_a), columns(row_b)], axis=1),
            jnp.concatenate([block_a, block_b], axis=0),
            preferred_element_type=F32,
        )
    row_c, block_c = weight_last
    total += jnp.dot(columns(row_c), block_c, preferred_element_type=F32)
    projected = total.astype(BF16)
    query_cols, key_cols = expert_query.shape[1], expert_key.shape[1]
    query = projected[:, :query_cols]
    action_key = projected[:, query_cols : query_cols + key_cols]
    action_value = projected[:, query_cols + key_cols :]

    later, _ = lax.optimization_barrier((expert_out, block_c))
    out_pairs, out_last = gather(later)
    piece = expert_out.shape[1]
    out_weight = jnp.zeros((expert_out.shape[0], piece * count), BF16)
    placed = [(mine, expert_out)]
    for row_a, block_a, row_b, block_b in out_pairs:
        placed += [(row_a, block_a), (row_b, block_b)]
    placed.append(out_last)
    for row, block in placed:
        out_weight = lax.dynamic_update_slice(out_weight, block, (zero, row * piece))

    attended = attend(
        prefix_length, action_length, query, prefix_keys, action_key, prefix_values, action_value
    )
    half = out_weight.shape[1] // 2

    def product(which):
        weight = cut(out_weight, which * half, half, 1)
        return jnp.dot(attended, weight, preferred_element_type=F32)

    sent = lax.ppermute(product(1 - col).astype(BF16), "col", swap)
    action_out = (product(col) + sent.astype(F32)).astype(BF16)
    return (prefix_keys, prefix_values, action_out)


def solution(mesh):
    placed = (
        P(("groups", "col"), "row"),
        P("row"),
        P("row", "col"),
        P("row", "col"),
        P(("groups", "row"), "col"),
        P("row", "col"),
        P("row", "col"),
        P("row", "col"),
        P("col", "row"),
        P(("groups", "row")),
        P(("groups", "row")),
    )
    return jax.shard_map(
        functools.partial(shards, mesh),
        mesh=mesh,
        in_specs=placed,
        out_specs=(
            P(("groups", "row"), "col"),
            P(("groups", "row"), "col"),
            P(("groups", "row"), "col"),
        ),
        check_vma=False,
    )
```

time: 437 us -> 233 us (0.53)
  waiting for transfers between devices: 303 us -> 62.5 us
  starting transfers between devices: 0.31 us -> 33 us
  Pallas kernels: 0 us -> 21.3 us
  matrix products: 68.4 us -> 50.1 us
  blocking collectives: 23.1 us -> 30.9 us
    all_gather x6 -> x0, waiting for transfers between devices: 206 us -> none  [the longest x1 67.7 us: shards(): lax.all_gather(expert_query, 'row', axis=0, tiled=True)]
    reduce_scatter x2 -> x0, waiting for transfers between devices: 94.1 us -> none  [the longest x1 79 us: shards(): lax.psum_scatter(jnp.dot(all_rows, joined, preferred_element_type=jnp.flo...]
    ppermute x0 -> x33, waiting for transfers between devices: none -> 62.5 us  [the longest x7 38.2 us: shards(): value_run = lax.ppermute(value_run.astype(BF16), 'row', back).astype(F32)]
    ppermute x0 -> x33, starting transfers between devices: none -> 33 us  [the longest x7 11.4 us: shards(): key_run = lax.ppermute(key_run.astype(BF16), 'row', ahead).astype(F32)]
    all_gather x0 -> x1, blocking collectives: none -> 30.9 us  [shards(): all_squares = lax.all_gather(squares, 'row', axis=0)]
    psum x1 -> x0, blocking collectives: 23.1 us -> none  [shards(): squares = lax.psum(jnp.sum(states * states, axis=1), 'row')]
    pallas_call x0 -> x1, Pallas kernels: none -> 21.3 us  [attend(): pl.pallas_call(functools.partial(attend_kernel, HEAD ** (-0.5) * math.log...]
    sub x2 -> x0, matrix products: 14.7 us -> none  [attend_block(): exponent = jnp.exp(scores - highest)]
  transfers between devices with their start and end apart: 8 -> 33, of which waited for: 8 -> 14; matrix products, arithmetic and copies ran while one was open for 18% -> 27% of each run, Pallas kernels for 0% -> 9%
where the time goes in v1:
time: 233 us
  waiting for transfers between devices  62.5 us (27%)
  matrix products  50.1 us (22%)
  starting transfers between devices  33 us (14%)
  blocking collectives  30.9 us (13%)
  Pallas kernels  21.3 us (9%)
  local copies, waits for them, and re-layouts  13.3 us (6%)
  between operations  11.9 us (5%)
  other arithmetic  9.52 us (4%)
    ppermute x7, waiting for transfers between devices, shards(): value_run = lax.ppermute(value_run.astype(BF16), 'row', back).astype(F32)  38.2 us
    all_gather x1, blocking collectives, shards(): all_squares = lax.all_gather(squares, 'row', axis=0)  30.9 us
    dot_general x3, matrix products, shards(): jnp.dot(jnp.concatenate([columns(row_a), columns(row_b)], axis=1), jnp.co...  28.8 us
    pallas_call x1, Pallas kernels, attend(): pl.pallas_call(functools.partial(attend_kernel, HEAD ** (-0.5) * math.log...  21.3 us
    ppermute x6, waiting for transfers between devices, gather(): ahead_block = lax.ppermute(ahead_block, 'row', ahead)  14.1 us
    ppermute x7, starting transfers between devices, shards(): key_run = lax.ppermute(key_run.astype(BF16), 'row', ahead).astype(F32)  11.4 us
    ppermute x6, starting transfers between devices, gather(): ahead_block = lax.ppermute(ahead_block, 'row', ahead)  10.2 us
    dot_general x2, matrix products, product(): return jnp.dot(attended, weight, preferred_element_type=F32)  9.62 us
  transfers between devices with their start and end apart: 33, of which 14 were waited for; matrix products, arithmetic and copies ran while one was open for 27% of the time, Pallas kernels for 9%

profile of v1, /device:TPU:0, one launch (start us, length us, event | category | flops | bytes accessed | tf_op | source)
XLA Modules:
  0.0 232.5 jit_solution(5634054088239696178)
XLA Ops:
  4.2 2.8 %collective-permute-start.16 = (bf16[256,2048]{1,0:T(8,128)(2,1)S(1)}, bf16[256,2048]{1,0:T(8,128)(2,1)}, u32[]{:S(2)}, u32[]{:S(2)}) collective-permute-start(bf16[256,2048]{1,0:T(8,128)(2,1)S(1)} %constant_dynamic-update-slice_fusion), channel_id=1, source_target_pairs={{0,4},{4,8},{8,12},{12,14},{14,10},{10,6},{6,2},{2,0},{1,5},{5,9},... | collective-permute-start | bytes 3145736 | tf_op jit(solution)/shard_map/ppermute | solution.py:113
  20.4 2.2 broadcast_select_fusion.3
  27.3 3.7 %collective-permute-done.16 = bf16[256,2048]{1,0:T(8,128)(2,1)} collective-permute-done((bf16[256,2048]{1,0:T(8,128)(2,1)S(1)}, bf16[256,2048]{1,0:T(8,128)(2,1)}, u32[]{:S(2)}, u32[]{:S(2)}) %collective-permute-start.16) | collective-permute-done | bytes 1048608 | tf_op jit(solution)/shard_map/ppermute | solution.py:113
  37.5 22.8 %collective-permute-done.9 = bf16[128,512]{1,0:T(8,128)(2,1)S(1)} collective-permute-done((bf16[128,512]{1,0:T(8,128)(2,1)S(1)}, bf16[128,512]{1,0:T(8,128)(2,1)S(1)}, u32[]{:S(2)}, u32[]{:S(2)}) %collective-permute-start.9) | collective-permute-done | bytes 131104 | tf_op jit(solution)/shard_map/ppermute | solution.py:152
  62.5 3.1 %collective-permute-done.10 = bf16[128,512]{1,0:T(8,128)(2,1)S(1)} collective-permute-done((bf16[128,512]{1,0:T(8,128)(2,1)S(1)}, bf16[128,512]{1,0:T(8,128)(2,1)S(1)}, u32[]{:S(2)}, u32[]{:S(2)}) %collective-permute-start.10) | collective-permute-done | bytes 131104 | tf_op jit(solution)/shard_map/ppermute | solution.py:152
  68.1 3.9 %collective-permute-done.11 = bf16[128,512]{1,0:T(8,128)(2,1)S(1)} collective-permute-done((bf16[128,512]{1,0:T(8,128)(2,1)S(1)}, bf16[128,512]{1,0:T(8,128)(2,1)S(1)}, u32[]{:S(2)}, u32[]{:S(2)}) %collective-permute-start.11) | collective-permute-done | bytes 131104 | tf_op jit(solution)/shard_map/ppermute | solution.py:152
  74.2 3.4 %collective-permute-done.12 = bf16[128,512]{1,0:T(8,128)(2,1)S(1)} collective-permute-done((bf16[128,512]{1,0:T(8,128)(2,1)S(1)}, bf16[128,512]{1,0:T(8,128)(2,1)S(1)}, u32[]{:S(2)}, u32[]{:S(2)}) %collective-permute-start.12) | collective-permute-done | bytes 131104 | tf_op jit(solution)/shard_map/ppermute | solution.py:152
  79.8 2.9 %collective-permute-done.13 = bf16[128,512]{1,0:T(8,128)(2,1)S(1)} collective-permute-done((bf16[128,512]{1,0:T(8,128)(2,1)S(1)}, bf16[128,512]{1,0:T(8,128)(2,1)S(1)}, u32[]{:S(2)}, u32[]{:S(2)}) %collective-permute-start.13) | collective-permute-done | bytes 131104 | tf_op jit(solution)/shard_map/ppermute | solution.py:152
  85.4 30.9 %all-gather = f32[8192]{0:T(1024)S(1)} all-gather(f32[1024]{0:T(1024)S(1)} %fusion.1), channel_id=2, replica_groups=mesh['groups'=2,'row'=8,'col'=2] {'row'}, dimensions={0}, use_global_device_ids=true | all-gather | bytes 36864 | tf_op jit(solution)/shard_map/all_gather | solution.py:139
  119.7 2.5 %broadcast_select_fusion = (bf16[1024,1024]{1,0:T(8,128)(2,1)S(1)}, bf16[1024,1024]{1,0:T(8,128)(2,1)S(1)}) fusion(bf16[1024,1024]{1,0:T(8,128)(2,1)} %collective-permute-done.15, bf16[1024,1024]{1,0:T(8,128)(2,1)} %param.16, pred[]{:T(512)S(6)} %eq.2), kind=kLoop, calls=%fused_computation.38 | loop fusion | flops 2097152 | bytes 8388609 | tf_op jit(solution)/shard_map/jit(_where)/select_n | solution.py:129
  122.2 4.5 %fusion.45 = f32[1024,2048]{1,0:T(8,128)} fusion(bf16[256,2048]{1,0:T(8,128)(2,1)S(1)} %copy-done.9, u32[]{:T(128)S(6)} %mul.166, bf16[1024,1024]{1,0:T(8,128)(2,1)S(1)} %get-tuple-element.14, bf16[1024,1024]{1,0:T(8,128)(2,1)S(1)} %get-tuple-element.13), kind=kOutput, calls=%fused_computation.63 | convolution fusion | flops 1074790400 | bytes 13631492 | tf_op jit(solution)/shard_map/dot_general | solution.py:166
  126.7 10.3 %collective-permute-done.20 = bf16[256,2048]{1,0:T(8,128)(2,1)S(1)} collective-permute-done((bf16[256,2048]{1,0:T(8,128)(2,1)}, bf16[256,2048]{1,0:T(8,128)(2,1)S(1)}, u32[]{:S(2)}, u32[]{:S(2)}) %collective-permute-start.20) | collective-permute-done | bytes 1048608 | tf_op jit(solution)/shard_map/ppermute | solution.py:113
  137.1 2.7 %fusion.41 = (bf16[1024,256]{1,0:T(8,128)(2,1)S(1)}, bf16[1024,256]{1,0:T(8,128)(2,1)S(1)}, bf16[1024,256]{1,0:T(8,128)(2,1)S(1)}, bf16[1024,256]{1,0:T(8,128)(2...) fusion(u32[]{:T(128)} %bitcast.12, bf16[1024,1024]{1,0:T(8,128)(2,1)S(1)} %get-tuple-element.14, ...), kind=kLoop, calls=%fused_computation.60 | loop fusion | flops 6291456 | bytes 7340056 | tf_op jit(solution)/shard_map/concatenate | solution.py:130
  139.9 2.3 collective-permute-start.23
  142.1 7.3 %fusion.6 = f32[1024,2048]{1,0:T(8,128)} fusion(bf16[256,2048]{1,0:T(8,128)(2,1)} %collective-permute-done.19, bf16[256,2048]{1,0:T(8,128)(2,1)} %collective-permute-done.18, bf16[1024,256]{1,0:T(8,128)(2,1)S(1)} %get-tuple-element.11, bf16[1024,256]{1,0:T(8,128)(2,1)S(1)} %get-tuple-element.10), kind=kOutput, calls=%fused_computation.27 | convolution fusion | flops 2153775104 | bytes 11534336 | tf_op jit(solution)/shard_map/dot_general | solution.py:168
  151.8 7.2 %fusion.2 = f32[1024,2048]{1,0:T(8,128)} fusion(bf16[256,2048]{1,0:T(8,128)(2,1)} %collective-permute-done.17, bf16[256,2048]{1,0:T(8,128)(2,1)} %collective-permute-done.16, bf16[1024,256]{1,0:T(8,128)(2,1)S(1)} %get-tuple-element.9, bf16[1024,256]{1,0:T(8,128)(2,1)S(1)} %get-tuple-element.8), kind=kOutput, calls=%fused_computation.23 | convolution fusion | flops 2153775104 | bytes 11534336 | tf_op jit(solution)/shard_map/dot_general | solution.py:168
  159.0 4.6 %fusion.43 = f32[1024,2048]{1,0:T(8,128)} fusion(bf16[256,2048]{1,0:T(8,128)(2,1)S(1)} %constant_dynamic-update-slice_fusion.3, u32[]{:T(128)} %bitcast.14, bf16[1024,1024]{1,0:T(8,128)(2,1)S(1)} %get-tuple-element.14, bf16[1024,1024]{1,0:T(8,128)(2,1)S(1)} %get-tuple-element.13), kind=kOutput, calls=%fused_computation.62 | convolution fusion | flops 1074790400 | bytes 13631492 | tf_op jit(solution)/shard_map/dot_general | solution.py:174
  165.6 14.4 %add_convert_fusion = bf16[1024,2048]{1,0:T(8,128)(2,1)} fusion(f32[1024,2048]{1,0:T(8,128)} %fusion.43, f32[1024,2048]{1,0:T(8,128)} %fusion.6, f32[1024,2048]{1,0:T(8,128)} %fusion.45, f32[1024,2048]{1,0:T(8,128)} %fusion.2, bf16[256,2048]{1,0:T(8,128)(2,1)S(1)} %collective-permute-done.21, bf16[256,2048]{1,0:T(8,128)(2,1)S(1)} %collective-permute-done.20, ...), kind=kOutput, calls=%fused_computation | convolution fusion | flops 2164260864 | bytes 40894464 | tf_op jit(solution)/shard_map/dot_general | solution.py:168
  185.1 21.3 %attend.1 = bf16[1024,1024]{1,0:T(8,128)(2,1)S(1)} custom-call(s32[1]{0:T(128)S(6)} %copy.26.plen_ref, s32[1]{0:T(128)S(6)} %copy.27.alen_ref, bf16[1024,1024]{1,0:T(8,128)(2,1)S(1)} %slice.84.q_ref, bf16[128,512]{1,0:T(8,128)(2,1)S(1)} %get-tuple-element.18.pk_ref, bf16[1024,512]{1,0:T(8,128)(2,1)S(1)} %get-tuple-element.6.ak_ref, ...), custom_call_target="tpu_custom_call" | custom-call | flops 9663676416 | bytes 4194304 | tf_op jit(solution)/shard_map/attend/pallas_call | solution.py:49
  213.4 2.8 %collective-permute-done.31 = bf16[512,256]{1,0:T(8,128)(2,1)S(1)} collective-permute-done((bf16[512,256]{1,0:T(8,128)(2,1)S(1)}, bf16[512,256]{1,0:T(8,128)(2,1)S(1)}, u32[]{:S(2)}, u32[]{:S(2)}) %collective-permute-start.31) | collective-permute-done | bytes 262176 | tf_op jit(solution)/shard_map/ppermute | solution.py:120
  216.2 2.1 collective-permute-done.30
  218.4 3.7 %fusion.17 = bf16[1024,1024]{1,0:T(8,128)(2,1)} fusion(bf16[1024,1024]{1,0:T(8,128)(2,1)S(1)} %attend.1, bf16[1024,2048]{1,0:T(8,128)(2,1)S(1)} %maximum_dynamic-update-slice_fusion, u32[]{:T(128)S(6)} %mul.182), kind=kOutput, calls=%fused_computation.40 | convolution fusion | flops 2148532224 | bytes 6291460 | tf_op jit(solution)/shard_map/dot_general | solution.py:199
  222.1 4.5 %collective-permute-done.32 = bf16[1024,1024]{1,0:T(8,128)(2,1)} collective-permute-done((bf16[1024,1024]{1,0:T(8,128)(2,1)}, bf16[1024,1024]{1,0:T(8,128)(2,1)}, u32[]{:S(2)}, u32[]{:S(2)}) %collective-permute-start.32) | collective-permute-done | bytes 2097184 | tf_op jit(solution)/shard_map/ppermute | solution.py:201
  226.6 6.0 %add_convert_fusion.1 = bf16[1024,1024]{1,0:T(8,128)(2,1)} fusion(bf16[1024,1024]{1,0:T(8,128)(2,1)} %collective-permute-done.32, bf16[1024,1024]{1,0:T(8,128)(2,1)S(1)} %attend.1, bf16[1024,2048]{1,0:T(8,128)(2,1)} %copy-done.7, u32[]{:T(128)S(6)} %mul.181), kind=kOutput, calls=%fused_computation.21 | convolution fusion | flops 2150629376 | bytes 8388612 | tf_op jit(solution)/shard_map/dot_general | solution.py:199
  (131 shorter events, 49.0 us)
Async XLA Ops:
  0.7 19.7 %collective-permute-start = (bf16[512,1024]{1,0:T(8,128)(2,1)}, bf16[512,1024]{1,0:T(8,128)(2,1)}, u32[]{:S(2)}, u32[]{:S(2)}) collective-permute-start(bf16[512,1024]{1,0:T(8,128)(2,1)} %param.12), channel_id=1, source_target_pairs={{0,1},{1,0},{2,3},{3,2},{4,5},{5,4},{6,7},{7,6},{8,9},{9,8},{10,11... | collective-permute-start | bytes 3145736 | tf_op jit(solution)/shard_map/ppermute | solution.py:127
  4.2 26.8 %collective-permute-start.16 = (bf16[256,2048]{1,0:T(8,128)(2,1)S(1)}, bf16[256,2048]{1,0:T(8,128)(2,1)}, u32[]{:S(2)}, u32[]{:S(2)}) collective-permute-start(bf16[256,2048]{1,0:T(8,128)(2,1)S(1)} %constant_dynamic-update-slice_fusion), channel_id=1, source_target_pairs={{0,4},{4,8},{8,12},{12,14},{14,10},{10,6},{6,2},{2,0},{1,5},{5,9},... | collective-permute-start | bytes 3145736 | tf_op jit(solution)/shard_map/ppermute | solution.py:113
  7.0 26.1 %collective-permute-start.17 = (bf16[256,2048]{1,0:T(8,128)(2,1)S(1)}, bf16[256,2048]{1,0:T(8,128)(2,1)}, u32[]{:S(2)}, u32[]{:S(2)}) collective-permute-start(bf16[256,2048]{1,0:T(8,128)(2,1)S(1)} %constant_dynamic-update-slice_fusion), channel_id=1, source_target_pairs={{4,0},{8,4},{12,8},{14,12},{10,14},{6,10},{2,6},{0,2},{5,1},{9,5},... | collective-permute-start | bytes 3145736 | tf_op jit(solution)/shard_map/ppermute | solution.py:114
  7.0 112.6 %collective-permute-start.15 = (bf16[1024,1024]{1,0:T(8,128)(2,1)}, bf16[1024,1024]{1,0:T(8,128)(2,1)}, u32[]{:S(2)}, u32[]{:S(2)}) collective-permute-start(bf16[1024,1024]{1,0:T(8,128)(2,1)} %param.16), channel_id=1, source_target_pairs={{0,1},{1,0},{2,3},{3,2},{4,5},{5,4},{6,7},{7,6},{8,9},{9,8},{10,11... | collective-permute-start | bytes 6291464 | tf_op jit(solution)/shard_map/ppermute | solution.py:127
  23.9 11.4 %collective-permute-start.8 = (bf16[128,512]{1,0:T(8,128)(2,1)S(1)}, bf16[128,512]{1,0:T(8,128)(2,1)S(1)}, u32[]{:S(2)}, u32[]{:S(2)}) collective-permute-start(bf16[128,512]{1,0:T(8,128)(2,1)S(1)} %dynamic-slice_convert_fusion), channel_id=1, source_target_pairs={{4,0},{8,4},{12,8},{14,12},{10,14},{6,10},{2,6},{0,2},{5,1},{9,5},... | collective-permute-start | bytes 393224 | tf_op jit(solution)/shard_map/ppermute | solution.py:152
  27.1 8.3 %collective-permute-start.1 = (bf16[128,512]{1,0:T(8,128)(2,1)S(1)}, bf16[128,512]{1,0:T(8,128)(2,1)S(1)}, u32[]{:S(2)}, u32[]{:S(2)}) collective-permute-start(bf16[128,512]{1,0:T(8,128)(2,1)S(1)} %dynamic-slice_convert_fusion.1), channel_id=1, source_target_pairs={{0,4},{4,8},{8,12},{12,14},{14,10},{10,6},{6,2},{2,0},{1,5},{5,9},... | collective-permute-start | bytes 393224 | tf_op jit(solution)/shard_map/ppermute | solution.py:151
  31.1 85.3 %collective-permute-start.18 = (bf16[256,2048]{1,0:T(8,128)(2,1)}, bf16[256,2048]{1,0:T(8,128)(2,1)}, u32[]{:S(2)}, u32[]{:S(2)}) collective-permute-start(bf16[256,2048]{1,0:T(8,128)(2,1)} %collective-permute-done.16), channel_id=1, source_target_pairs={{0,4},{4,8},{8,12},{12,14},{14,10},{10,6},{6,2},{2,0},{1,5},{5,9},... | collective-permute-start | bytes 3145736 | tf_op jit(solution)/shard_map/ppermute | solution.py:113
  33.1 84.4 %collective-permute-start.19 = (bf16[256,2048]{1,0:T(8,128)(2,1)}, bf16[256,2048]{1,0:T(8,128)(2,1)}, u32[]{:S(2)}, u32[]{:S(2)}) collective-permute-start(bf16[256,2048]{1,0:T(8,128)(2,1)} %collective-permute-done.17), channel_id=1, source_target_pairs={{4,0},{8,4},{12,8},{14,12},{10,14},{6,10},{2,6},{0,2},{5,1},{9,5},... | collective-permute-start | bytes 3145736 | tf_op jit(solution)/shard_map/ppermute | solution.py:114
  35.3 25.0 %collective-permute-start.9 = (bf16[128,512]{1,0:T(8,128)(2,1)S(1)}, bf16[128,512]{1,0:T(8,128)(2,1)S(1)}, u32[]{:S(2)}, u32[]{:S(2)}) collective-permute-start(bf16[128,512]{1,0:T(8,128)(2,1)S(1)} %add_convert_fusion.7), channel_id=1, source_target_pairs={{4,0},{8,4},{12,8},{14,12},{10,14},{6,10},{2,6},{0,2},{5,1},{9,5},... | collective-permute-start | bytes 393224 | tf_op jit(solution)/shard_map/ppermute | solution.py:152
  35.5 25.1 %collective-permute-start.2 = (bf16[128,512]{1,0:T(8,128)(2,1)S(1)}, bf16[128,512]{1,0:T(8,128)(2,1)S(1)}, u32[]{:S(2)}, u32[]{:S(2)}) collective-permute-start(bf16[128,512]{1,0:T(8,128)(2,1)S(1)} %add_convert_fusion.13), channel_id=1, source_target_pairs={{0,4},{4,8},{8,12},{12,14},{14,10},{10,6},{6,2},{2,0},{1,5},{5,9},... | collective-permute-start | bytes 393224 | tf_op jit(solution)/shard_map/ppermute | solution.py:151
  82.7 33.7 %collective-permute-start.14 = (bf16[128,512]{1,0:T(8,128)(2,1)S(1)}, bf16[128,512]{1,0:T(8,128)(2,1)S(1)}, u32[]{:S(2)}, u32[]{:S(2)}) collective-permute-start(bf16[128,512]{1,0:T(8,128)(2,1)S(1)} %add_convert_fusion.2), channel_id=1, source_target_pairs={{4,0},{8,4},{12,8},{14,12},{10,14},{6,10},{2,6},{0,2},{5,1},{9,5},... | collective-permute-start | bytes 393224 | tf_op jit(solution)/shard_map/ppermute | solution.py:152
  83.1 33.3 %collective-permute-start.7 = (bf16[128,512]{1,0:T(8,128)(2,1)S(1)}, bf16[128,512]{1,0:T(8,128)(2,1)S(1)}, u32[]{:S(2)}, u32[]{:S(2)}) collective-permute-start(bf16[128,512]{1,0:T(8,128)(2,1)S(1)} %add_convert_fusion.8), channel_id=1, source_target_pairs={{0,4},{4,8},{8,12},{12,14},{14,10},{10,6},{6,2},{2,0},{1,5},{5,9},... | collective-permute-start | bytes 393224 | tf_op jit(solution)/shard_map/ppermute | solution.py:151
  116.4 20.6 %collective-permute-start.20 = (bf16[256,2048]{1,0:T(8,128)(2,1)}, bf16[256,2048]{1,0:T(8,128)(2,1)S(1)}, u32[]{:S(2)}, u32[]{:S(2)}) collective-permute-start(bf16[256,2048]{1,0:T(8,128)(2,1)} %collective-permute-done.18), channel_id=1, source_target_pairs={{0,4},{4,8},{8,12},{12,14},{14,10},{10,6},{6,2},{2,0},{1,5},{5,9},... | collective-permute-start | bytes 3145736 | tf_op jit(solution)/shard_map/ppermute | solution.py:113
  117.6 22.2 %collective-permute-start.21 = (bf16[256,2048]{1,0:T(8,128)(2,1)}, bf16[256,2048]{1,0:T(8,128)(2,1)S(1)}, u32[]{:S(2)}, u32[]{:S(2)}) collective-permute-start(bf16[256,2048]{1,0:T(8,128)(2,1)} %collective-permute-done.19), channel_id=1, source_target_pairs={{4,0},{8,4},{12,8},{14,12},{10,14},{6,10},{2,6},{0,2},{5,1},{9,5},... | collective-permute-start | bytes 3145736 | tf_op jit(solution)/shard_map/ppermute | solution.py:114
  137.1 12.3 %collective-permute-start.22 = (bf16[128,2048]{1,0:T(8,128)(2,1)S(1)}, bf16[128,2048]{1,0:T(8,128)(2,1)S(1)}, u32[]{:S(2)}, u32[]{:S(2)}) collective-permute-start(bf16[128,2048]{1,0:T(8,128)(2,1)S(1)} %slice.82), channel_id=1, source_target_pairs={{0,4},{4,8},{8,12},{12,14},{14,10},{10,6},{6,2},{2,0},{1,5},{5,9},... | collective-permute-start | bytes 1572872 | tf_op jit(solution)/shard_map/ppermute | solution.py:119
  139.9 9.8 %collective-permute-start.23 = (bf16[128,2048]{1,0:T(8,128)(2,1)S(1)}, bf16[128,2048]{1,0:T(8,128)(2,1)S(1)}, u32[]{:S(2)}, u32[]{:S(2)}) collective-permute-start(bf16[128,2048]{1,0:T(8,128)(2,1)S(1)} %slice.83), channel_id=1, source_target_pairs={{4,0},{8,4},{12,8},{14,12},{10,14},{6,10},{2,6},{0,2},{5,1},{9,5},... | collective-permute-start | bytes 1572872 | tf_op jit(solution)/shard_map/ppermute | solution.py:120
  149.7 13.8 %collective-permute-start.24 = (bf16[1024,256]{1,0:T(8,128)(2,1)S(1)}, bf16[1024,256]{1,0:T(8,128)(2,1)}, u32[]{:S(2)}, u32[]{:S(2)}) collective-permute-start(bf16[1024,256]{1,0:T(8,128)(2,1)S(1)} %copy-done.14), channel_id=1, source_target_pairs={{0,4},{4,8},{8,12},{12,14},{14,10},{10,6},{6,2},{2,0},{1,5},{5,9},... | collective-permute-start | bytes 1572872 | tf_op jit(solution)/shard_map/ppermute | solution.py:113
  151.5 13.8 %collective-permute-start.25 = (bf16[1024,256]{1,0:T(8,128)(2,1)S(1)}, bf16[1024,256]{1,0:T(8,128)(2,1)}, u32[]{:S(2)}, u32[]{:S(2)}) collective-permute-start(bf16[1024,256]{1,0:T(8,128)(2,1)S(1)} %copy-done.14), channel_id=1, source_target_pairs={{4,0},{8,4},{12,8},{14,12},{10,14},{6,10},{2,6},{0,2},{5,1},{9,5},... | collective-permute-start | bytes 1572872 | tf_op jit(solution)/shard_map/ppermute | solution.py:114
  163.6 19.4 %collective-permute-start.26 = (bf16[1024,256]{1,0:T(8,128)(2,1)}, bf16[1024,256]{1,0:T(8,128)(2,1)}, u32[]{:S(2)}, u32[]{:S(2)}) collective-permute-start(bf16[1024,256]{1,0:T(8,128)(2,1)} %collective-permute-done.24), channel_id=1, source_target_pairs={{0,4},{4,8},{8,12},{12,14},{14,10},{10,6},{6,2},{2,0},{1,5},{5,9},... | collective-permute-start | bytes 1572872 | tf_op jit(solution)/shard_map/ppermute | solution.py:113
  165.3 19.5 %collective-permute-start.27 = (bf16[1024,256]{1,0:T(8,128)(2,1)}, bf16[1024,256]{1,0:T(8,128)(2,1)}, u32[]{:S(2)}, u32[]{:S(2)}) collective-permute-start(bf16[1024,256]{1,0:T(8,128)(2,1)} %collective-permute-done.25), channel_id=1, source_target_pairs={{4,0},{8,4},{12,8},{14,12},{10,14},{6,10},{2,6},{0,2},{5,1},{9,5},... | collective-permute-start | bytes 1572872 | tf_op jit(solution)/shard_map/ppermute | solution.py:114
  183.0 28.7 %collective-permute-start.28 = (bf16[1024,256]{1,0:T(8,128)(2,1)}, bf16[1024,256]{1,0:T(8,128)(2,1)S(1)}, u32[]{:S(2)}, u32[]{:S(2)}) collective-permute-start(bf16[1024,256]{1,0:T(8,128)(2,1)} %collective-permute-done.26), channel_id=1, source_target_pairs={{0,4},{4,8},{8,12},{12,14},{14,10},{10,6},{6,2},{2,0},{1,5},{5,9},... | collective-permute-start | bytes 1572872 | tf_op jit(solution)/shard_map/ppermute | solution.py:113
  184.8 24.9 %collective-permute-start.29 = (bf16[1024,256]{1,0:T(8,128)(2,1)}, bf16[1024,256]{1,0:T(8,128)(2,1)S(1)}, u32[]{:S(2)}, u32[]{:S(2)}) collective-permute-start(bf16[1024,256]{1,0:T(8,128)(2,1)} %collective-permute-done.27), channel_id=1, source_target_pairs={{4,0},{8,4},{12,8},{14,12},{10,14},{6,10},{2,6},{0,2},{5,1},{9,5},... | collective-permute-start | bytes 1572872 | tf_op jit(solution)/shard_map/ppermute | solution.py:114
  209.7 6.4 %collective-permute-start.31 = (bf16[512,256]{1,0:T(8,128)(2,1)S(1)}, bf16[512,256]{1,0:T(8,128)(2,1)S(1)}, u32[]{:S(2)}, u32[]{:S(2)}) collective-permute-start(bf16[512,256]{1,0:T(8,128)(2,1)S(1)} %slice.88), channel_id=1, source_target_pairs={{4,0},{8,4},{12,8},{14,12},{10,14},{6,10},{2,6},{0,2},{5,1},{9,5},... | collective-permute-start | bytes 786440 | tf_op jit(solution)/shard_map/ppermute | solution.py:120
  211.7 6.6 %collective-permute-start.30 = (bf16[512,256]{1,0:T(8,128)(2,1)S(1)}, bf16[512,256]{1,0:T(8,128)(2,1)S(1)}, u32[]{:S(2)}, u32[]{:S(2)}) collective-permute-start(bf16[512,256]{1,0:T(8,128)(2,1)S(1)} %slice.87), channel_id=1, source_target_pairs={{0,4},{4,8},{8,12},{12,14},{14,10},{10,6},{6,2},{2,0},{1,5},{5,9},... | collective-permute-start | bytes 786440 | tf_op jit(solution)/shard_map/ppermute | solution.py:119
  (26 other events, 418.3 us)

commit v2 on v1

--- a/solution.py
+++ b/solution.py
@@ -136,7 +136,14 @@
     wide = states.astype(F32)
     squares = jnp.sum(wide * wide, axis=1)
     features = prefix_states.shape[1] * count
-    all_squares = lax.all_gather(squares, "row", axis=0)
+    if count & (count - 1):
+        squares = lax.psum(squares, "row")
+    else:
+        hop = 1
+        while hop < count:
+            pairs = [(r, r ^ hop) for r in range(count)]
+            squares += lax.ppermute(squares, "row", pairs)
+            hop *= 2
     scaled = (wide * prefix_gain[None, :]).astype(BF16)
     key_part = jnp.dot(scaled, backbone_key, preferred_element_type=F32)
     value_part = jnp.dot(scaled, backbone_value, preferred_element_type=F32)
@@ -148,30 +155,41 @@
     key_run = part(key_part, row_at(-1))
     value_run = part(value_part, row_at(1))
     for step in range(count - 1):
+        if step == 2 and len(weight_pairs) > 2:
+            key_run, value_run, _, _ = lax.optimization_barrier(
+                (key_run, value_run, weight_pairs[1][1], weight_pairs[1][3])
+            )
         key_run = lax.ppermute(key_run.astype(BF16), "row", ahead).astype(F32)
         value_run = lax.ppermute(value_run.astype(BF16), "row", back).astype(F32)
         key_run += part(key_part, row_at(-2 - step))
         value_run += part(value_part, row_at(2 + step - count))
-    own_squares = lax.dynamic_slice(jnp.sum(all_squares, axis=0), (mine * own,), (own,))
+    own_squares = lax.dynamic_slice(squares, (mine * own,), (own,))
     row_scale = lax.rsqrt(own_squares / features + 1e-06)[:, None]
     prefix_keys = (key_run * row_scale).astype(BF16)
     prefix_values = (value_run * row_scale).astype(BF16)
 
+    action_states, states = lax.optimization_barrier((action_states, states))
     actions = both(action_states, 1)
     depth = joined.shape[0]
 
     def columns(row):
         return cut(actions, row * depth, depth, 1)
 
-    total = jnp.dot(columns(mine), joined, preferred_element_type=F32)
+    row_c, block_c = weight_last
+    blocks = [(mine, joined)]
     for row_a, block_a, row_b, block_b in weight_pairs:
-        total += jnp.dot(
-            jnp.concatenate([columns(row_a), columns(row_b)], axis=1),
-            jnp.concatenate([block_a, block_b], axis=0),
+        blocks += [(row_a, block_a), (row_b, block_b)]
+    blocks.append((row_c, block_c))
+    early = max(1, len(blocks) - 3)
+
+    def product_of(some):
+        return jnp.dot(
+            jnp.concatenate([columns(row) for row, _ in some], axis=1),
+            jnp.concatenate([block for _, block in some], axis=0),
             preferred_element_type=F32,
         )
-    row_c, block_c = weight_last
-    total += jnp.dot(columns(row_c), block_c, preferred_element_type=F32)
+
+    total = lax.optimization_barrier(product_of(blocks[:early])) + product_of(blocks[early:])
     projected = total.astype(BF16)
     query_cols, key_cols = expert_query.shape[1], expert_key.shape[1]
     query = projected[:, :query_cols]
@@ -198,8 +216,10 @@
         weight = cut(out_weight, which * half, half, 1)
         return jnp.dot(attended, weight, preferred_element_type=F32)
 
-    sent = lax.ppermute(product(1 - col).astype(BF16), "col", swap)
-    action_out = (product(col) + sent.astype(F32)).astype(BF16)
+    away = product(1 - col).astype(BF16)
+    sent = lax.ppermute(away, "col", swap)
+    kept = lax.optimization_barrier(product(col))
+    action_out = (kept + sent.astype(F32)).astype(BF16)
     return (prefix_keys, prefix_values, action_out)
 
 

time: 233 us -> 222 us (0.953)
  blocking collectives: 30.9 us -> 0 us
  waiting for transfers between devices: 62.5 us -> 87.1 us
  matrix products: 50.1 us -> 26.5 us
  starting transfers between devices: 33 us -> 47.5 us
  local copies, waits for them, and re-layouts: 13.3 us -> 17.9 us
    all_gather x1 -> x0, blocking collectives: 30.9 us -> none  [shards(): all_squares = lax.all_gather(squares, 'row', axis=0)]
    ppermute x7, waiting for transfers between devices: 38.2 us -> 12.1 us  [shards(): value_run = lax.ppermute(value_run.astype(BF16), 'row', back).astype(F32)]
    ppermute x7, waiting for transfers between devices: 0.52 us -> 23.5 us  [shards(): key_run = lax.ppermute(key_run.astype(BF16), 'row', ahead).astype(F32)]
    dot_general x5 -> x2, matrix products: 37.9 us -> 16.3 us  [product_of(): jnp.dot(jnp.concatenate([columns(row) for row, _ in some], axis=1), jnp.c...]
    ppermute x1 -> x4, waiting for transfers between devices: 4.5 us -> 25.1 us  [the longest x3 24.6 us: shards(): squares += lax.ppermute(squares, 'row', pairs)]
    ppermute x2, waiting for transfers between devices: 3.07 us -> 17.6 us  [gather(): lax.ppermute(back_block[half:], 'row', back)]
    ppermute x6, waiting for transfers between devices: 14.1 us -> 5.6 us  [gather(): ahead_block = lax.ppermute(ahead_block, 'row', ahead)]
    unnamed x37 -> x26, local copies, waits for them, and re-layouts: 3.56 us -> 11.9 us
  transfers between devices with their start and end apart: 33 -> 36, of which waited for: 14 -> 13; matrix products, arithmetic and copies ran while one was open for 27% -> 18% of each run, Pallas kernels for 9% -> 0%
where the time goes in v2:
time: 222 us; the launch traced here: 221 us
  waiting for transfers between devices  87.1 us (39%)
  starting transfers between devices  47.5 us (21%)
  matrix products  26.5 us (12%)
  Pallas kernels  21.3 us (10%)
  local copies, waits for them, and re-layouts  17.9 us (8%)
  between operations  11.9 us (5%)
  other arithmetic  9.11 us (4%)
    ppermute x3, waiting for transfers between devices, shards(): squares += lax.ppermute(squares, 'row', pairs)  24.6 us
    ppermute x7, waiting for transfers between devices, shards(): key_run = lax.ppermute(key_run.astype(BF16), 'row', ahead).astype(F32)  23.5 us
    pallas_call x1, Pallas kernels, attend(): pl.pallas_call(functools.partial(attend_kernel, HEAD ** (-0.5) * math.log...  21.3 us
    ppermute x2, waiting for transfers between devices, gather(): lax.ppermute(back_block[half:], 'row', back)  17.6 us
    ppermute x6, starting transfers between devices, gather(): ahead_block = lax.ppermute(ahead_block, 'row', ahead)  16.7 us
    dot_general x2, matrix products, product_of(): jnp.dot(jnp.concatenate([columns(row) for row, _ in some], axis=1), jnp.c...  16.3 us
    ppermute x7, starting transfers between devices, shards(): key_run = lax.ppermute(key_run.astype(BF16), 'row', ahead).astype(F32)  13 us
    ppermute x7, waiting for transfers between devices, shards(): value_run = lax.ppermute(value_run.astype(BF16), 'row', back).astype(F32)  12.1 us
  transfers between devices with their start and end apart: 36, of which 13 were waited for; matrix products, arithmetic and copies ran while one was open for 18% of the time, Pallas kernels for 0%

profile of v2, /device:TPU:0, one launch (start us, length us, event | category | flops | bytes accessed | tf_op | source)
XLA Modules:
  0.0 221.4 jit_solution(12223588495285465129)
XLA Ops:
  1.2 2.6 %collective-permute-start.27 = (bf16[1024,256]{1,0:T(8,128)(2,1)}, bf16[1024,256]{1,0:T(8,128)(2,1)}, u32[]{:S(2)}, u32[]{:S(2)}) collective-permute-start(bf16[1024,256]{1,0:T(8,128)(2,1)} %param.20), channel_id=1, source_target_pairs={{0,4},{4,8},{8,12},{12,14},{14,10},{10,6},{6,2},{2,0},{1,5},{5,9},... | collective-permute-start | bytes 1572872 | tf_op jit(solution)/shard_map/ppermute | solution.py:113
  33.7 5.6 %collective-permute-done.5 = bf16[256,2048]{1,0:T(8,128)(2,1)} collective-permute-done((bf16[256,2048]{1,0:T(8,128)(2,1)}, bf16[256,2048]{1,0:T(8,128)(2,1)}, u32[]{:S(2)}, u32[]{:S(2)}) %collective-permute-start.5) | collective-permute-done | bytes 1048608 | tf_op jit(solution)/shard_map/ppermute | solution.py:113
  41.3 2.3 %constant_dynamic-update-slice_fusion.6 = bf16[1280,2048]{1,0:T(8,128)(2,1)} fusion(bf16[1280,2048]{1,0:T(8,128)(2,1)} %get-tuple-element.21, bf16[256,2048]{1,0:T(8,128)(2,1)} %collective-permute-done.5), kind=kLoop, calls=%fused_computation.83 | loop fusion | bytes 2097152
  47.5 5.0 %collective-permute-done.14 = f32[1024]{0:T(1024)S(1)} collective-permute-done((f32[1024]{0:T(1024)S(1)}, f32[1024]{0:T(1024)S(1)}, u32[]{:S(2)}, u32[]{:S(2)}) %collective-permute-start.14) | collective-permute-done | bytes 4128 | tf_op jit(solution)/shard_map/ppermute | solution.py:145
  52.6 3.5 %collective-permute-done.15 = f32[1024]{0:T(1024)S(1)} collective-permute-done((f32[1024]{0:T(1024)S(1)}, f32[1024]{0:T(1024)S(1)}, u32[]{:S(2)}, u32[]{:S(2)}) %collective-permute-start.15) | collective-permute-done | bytes 4128 | tf_op jit(solution)/shard_map/ppermute | solution.py:145
  57.9 5.9 %collective-permute-start.16 = (f32[1024]{0:T(1024)S(1)}, f32[1024]{0:T(1024)S(1)}, u32[]{:S(2)}, u32[]{:S(2)}) collective-permute-start(f32[1024]{0:T(1024)S(1)} %add.73), channel_id=1, source_target_pairs={{0,8},{2,10},{4,12},{6,14},{8,0},{10,2},{12,4},{14,6},{1,9},{3,11}... | collective-permute-start | bytes 12296 | tf_op jit(solution)/shard_map/ppermute | solution.py:145
  63.8 16.1 %collective-permute-done.16 = f32[1024]{0:T(1024)S(1)} collective-permute-done((f32[1024]{0:T(1024)S(1)}, f32[1024]{0:T(1024)S(1)}, u32[]{:S(2)}, u32[]{:S(2)}) %collective-permute-start.16) | collective-permute-done | bytes 4128 | tf_op jit(solution)/shard_map/ppermute | solution.py:145
  79.9 5.9 %collective-permute-start.31 = (bf16[1024,256]{1,0:T(8,128)(2,1)S(1)}, bf16[1024,256]{1,0:T(8,128)(2,1)S(1)}, u32[]{:S(2)}, u32[]{:S(2)}) collective-permute-start(bf16[1024,256]{1,0:T(8,128)(2,1)S(1)} %collective-permute-done.29), channel_id=1, source_target_pairs={{0,4},{4,8},{8,12},{12,14},{14,10},{10,6},{6,2},{2,0},{1,5},{5,9},... | collective-permute-start | bytes 1572872 | tf_op jit(solution)/shard_map/ppermute | solution.py:113
  87.4 11.5 %collective-permute-done.4 = bf16[128,512]{1,0:T(8,128)(2,1)S(1)} collective-permute-done((bf16[128,512]{1,0:T(8,128)(2,1)S(1)}, bf16[128,512]{1,0:T(8,128)(2,1)S(1)}, u32[]{:S(2)}, u32[]{:S(2)}) %collective-permute-start.4) | collective-permute-done | bytes 131104 | tf_op jit(solution)/shard_map/ppermute | solution.py:163
  98.8 2.3 %collective-permute-start.2 = (bf16[128,512]{1,0:T(8,128)(2,1)S(1)}, bf16[128,512]{1,0:T(8,128)(2,1)S(1)}, u32[]{:S(2)}, u32[]{:S(2)}) collective-permute-start(bf16[128,512]{1,0:T(8,128)(2,1)S(1)} %add_convert_fusion.11), channel_id=1, source_target_pairs={{0,4},{4,8},{8,12},{12,14},{14,10},{10,6},{6,2},{2,0},{1,5},{5,9},... | collective-permute-start | bytes 393224 | tf_op jit(solution)/shard_map/ppermute | solution.py:162
  101.3 3.0 %collective-permute-start.33 = (bf16[512,256]{1,0:T(8,128)(2,1)S(1)}, bf16[512,256]{1,0:T(8,128)(2,1)S(1)}, u32[]{:S(2)}, u32[]{:S(2)}) collective-permute-start(bf16[512,256]{1,0:T(8,128)(2,1)S(1)} %slice.87), channel_id=1, source_target_pairs={{0,4},{4,8},{8,12},{12,14},{14,10},{10,6},{6,2},{2,0},{1,5},{5,9},... | collective-permute-start | bytes 786440 | tf_op jit(solution)/shard_map/ppermute | solution.py:119
  105.0 3.2 %collective-permute-done.33 = bf16[512,256]{1,0:T(8,128)(2,1)S(1)} collective-permute-done((bf16[512,256]{1,0:T(8,128)(2,1)S(1)}, bf16[512,256]{1,0:T(8,128)(2,1)S(1)}, u32[]{:S(2)}, u32[]{:S(2)}) %collective-permute-start.33) | collective-permute-done | bytes 262176 | tf_op jit(solution)/shard_map/ppermute | solution.py:119
  108.2 17.6 %collective-permute-done.34 = bf16[512,256]{1,0:T(8,128)(2,1)S(1)} collective-permute-done((bf16[512,256]{1,0:T(8,128)(2,1)S(1)}, bf16[512,256]{1,0:T(8,128)(2,1)S(1)}, u32[]{:S(2)}, u32[]{:S(2)}) %collective-permute-start.34) | collective-permute-done | bytes 262176 | tf_op jit(solution)/shard_map/ppermute | solution.py:120
  130.2 2.4 %collective-permute-start.23 = (bf16[256,2048]{1,0:T(8,128)(2,1)S(1)}, bf16[256,2048]{1,0:T(8,128)(2,1)S(1)}, u32[]{:S(2)}, u32[]{:S(2)}) collective-permute-start(bf16[256,2048]{1,0:T(8,128)(2,1)S(1)} %collective-permute-done.6), channel_id=1, source_target_pairs={{0,4},{4,8},{8,12},{12,14},{14,10},{10,6},{6,2},{2,0},{1,5},{5,9},... | collective-permute-start | bytes 3145736 | tf_op jit(solution)/shard_map/ppermute | solution.py:113
  137.7 15.8 %collective-permute-done.10 = bf16[128,512]{1,0:T(8,128)(2,1)S(1)} collective-permute-done((bf16[128,512]{1,0:T(8,128)(2,1)S(1)}, bf16[128,512]{1,0:T(8,128)(2,1)S(1)}, u32[]{:S(2)}, u32[]{:S(2)}) %collective-permute-start.10) | collective-permute-done | bytes 131104 | tf_op jit(solution)/shard_map/ppermute | solution.py:162
  153.5 2.5 %collective-permute-start.11 = (bf16[128,512]{1,0:T(8,128)(2,1)S(1)}, bf16[128,512]{1,0:T(8,128)(2,1)S(1)}, u32[]{:S(2)}, u32[]{:S(2)}) collective-permute-start(bf16[128,512]{1,0:T(8,128)(2,1)S(1)} %add_convert_fusion.8), channel_id=1, source_target_pairs={{0,4},{4,8},{8,12},{12,14},{14,10},{10,6},{6,2},{2,0},{1,5},{5,9},... | collective-permute-start | bytes 393224 | tf_op jit(solution)/shard_map/ppermute | solution.py:162
  156.1 3.8 %collective-permute-done.11 = bf16[128,512]{1,0:T(8,128)(2,1)S(1)} collective-permute-done((bf16[128,512]{1,0:T(8,128)(2,1)S(1)}, bf16[128,512]{1,0:T(8,128)(2,1)S(1)}, u32[]{:S(2)}, u32[]{:S(2)}) %collective-permute-start.11) | collective-permute-done | bytes 131104 | tf_op jit(solution)/shard_map/ppermute | solution.py:162
  162.6 3.9 %collective-permute-done.12 = bf16[128,512]{1,0:T(8,128)(2,1)S(1)} collective-permute-done((bf16[128,512]{1,0:T(8,128)(2,1)S(1)}, bf16[128,512]{1,0:T(8,128)(2,1)S(1)}, u32[]{:S(2)}, u32[]{:S(2)}) %collective-permute-start.12) | collective-permute-done | bytes 131104 | tf_op jit(solution)/shard_map/ppermute | solution.py:162
  171.3 10.3 %fusion.46 = f32[1024,2048]{1,0:T(8,128)} fusion(bf16[1024,1280]{1,0:T(8,128)(2,1)S(1)} %fusion.40, bf16[1280,2048]{1,0:T(8,128)(2,1)} %constant_dynamic-update-slice_fusion.3), kind=kOutput, calls=%fused_computation.101 | convolution fusion | flops 5368709120 | bytes 16252928 | tf_op jit(solution)/shard_map/dot_general | solution.py:186
  181.7 6.0 %add_convert_fusion = bf16[1024,2048]{1,0:T(8,128)(2,1)S(1)} fusion(f32[1024,2048]{1,0:T(8,128)} %fusion.46, bf16[128,2048]{1,0:T(8,128)(2,1)S(1)} %collective-permute-done.26, bf16[128,2048]{1,0:T(8,128)(2,1)S(1)} %collective-permute-done.25, bf16[256,2048]{1,0:T(8,128)(2,1)S(1)} %collective-permute-done.24, ...), kind=kOutput, calls=%fused_computation | convolution fusion | flops 3242721280 | bytes 17301504 | tf_op jit(solution)/shard_map/dot_general | solution.py:186
  188.1 21.3 %attend.1 = bf16[1024,1024]{1,0:T(8,128)(2,1)S(1)} custom-call(s32[1]{0:T(128)S(6)} %copy.35.plen_ref, s32[1]{0:T(128)S(6)} %copy.36.alen_ref, bf16[1024,1024]{1,0:T(8,128)(2,1)S(1)} %slice.84.q_ref, bf16[128,512]{1,0:T(8,128)(2,1)S(1)} %get-tuple-element.26.pk_ref, bf16[1024,512]{1,0:T(8,128)(2,1)S(1)} %get-tuple-element.10.ak_ref, ...), custom_call_target="tpu_custom_call" | custom-call | flops 9663676416 | bytes 4194304 | tf_op jit(solution)/shard_map/attend/pallas_call | solution.py:49
  209.5 3.7 %fusion.16 = bf16[1024,1024]{1,0:T(8,128)(2,1)} fusion(bf16[1024,1024]{1,0:T(8,128)(2,1)S(1)} %attend.1, bf16[1024,2048]{1,0:T(8,128)(2,1)S(1)} %maximum_dynamic-update-slice_fusion, u32[]{:T(128)S(6)} %mul.182), kind=kOutput, calls=%fused_computation.37 | convolution fusion | flops 2148532224 | bytes 6291460 | tf_op jit(solution)/shard_map/dot_general | solution.py:217
  213.1 4.0 %fusion.14 = f32[1024,1024]{1,0:T(8,128)S(1)} fusion(bf16[1024,1024]{1,0:T(8,128)(2,1)S(1)} %attend.1, bf16[1024,2048]{1,0:T(8,128)(2,1)} %copy-done.4, u32[]{:T(128)S(6)} %mul.181), kind=kOutput, calls=%fused_computation.33 | convolution fusion | flops 2147483648 | bytes 8388612 | tf_op jit(solution)/shard_map/dot_general | solution.py:217
  217.6 3.8 %add_convert_fusion.1 = bf16[1024,1024]{1,0:T(8,128)(2,1)} fusion(f32[1024,1024]{1,0:T(8,128)S(1)} %fusion.14, bf16[1024,1024]{1,0:T(8,128)(2,1)} %collective-permute-done.35), kind=kLoop, calls=%fused_computation.21 | loop fusion | flops 3145728 | bytes 8388608 | tf_op jit(solution)/shard_map/convert_element_type | solution.py:222
  (127 shorter events, 47.6 us)
Async XLA Ops:
  0.7 28.6 %collective-permute-start = (bf16[512,1024]{1,0:T(8,128)(2,1)}, bf16[512,1024]{1,0:T(8,128)(2,1)}, u32[]{:S(2)}, u32[]{:S(2)}) collective-permute-start(bf16[512,1024]{1,0:T(8,128)(2,1)} %param.12), channel_id=1, source_target_pairs={{0,1},{1,0},{2,3},{3,2},{4,5},{5,4},{6,7},{7,6},{8,9},{9,8},{10,11... | collective-permute-start | bytes 3145736 | tf_op jit(solution)/shard_map/ppermute | solution.py:127
  1.2 23.6 %collective-permute-start.27 = (bf16[1024,256]{1,0:T(8,128)(2,1)}, bf16[1024,256]{1,0:T(8,128)(2,1)}, u32[]{:S(2)}, u32[]{:S(2)}) collective-permute-start(bf16[1024,256]{1,0:T(8,128)(2,1)} %param.20), channel_id=1, source_target_pairs={{0,4},{4,8},{8,12},{12,14},{14,10},{10,6},{6,2},{2,0},{1,5},{5,9},... | collective-permute-start | bytes 1572872 | tf_op jit(solution)/shard_map/ppermute | solution.py:113
  3.8 22.2 %collective-permute-start.28 = (bf16[1024,256]{1,0:T(8,128)(2,1)}, bf16[1024,256]{1,0:T(8,128)(2,1)}, u32[]{:S(2)}, u32[]{:S(2)}) collective-permute-start(bf16[1024,256]{1,0:T(8,128)(2,1)} %param.20), channel_id=1, source_target_pairs={{4,0},{8,4},{12,8},{14,12},{10,14},{6,10},{2,6},{0,2},{5,1},{9,5},... | collective-permute-start | bytes 1572872 | tf_op jit(solution)/shard_map/ppermute | solution.py:114
  9.5 29.8 %collective-permute-start.5 = (bf16[256,2048]{1,0:T(8,128)(2,1)}, bf16[256,2048]{1,0:T(8,128)(2,1)}, u32[]{:S(2)}, u32[]{:S(2)}) collective-permute-start(bf16[256,2048]{1,0:T(8,128)(2,1)} %get-tuple-element.22), channel_id=1, source_target_pairs={{0,4},{4,8},{8,12},{12,14},{14,10},{10,6},{6,2},{2,0},{1,5},{5,9},... | collective-permute-start | bytes 3145736 | tf_op jit(solution)/shard_map/ppermute | solution.py:113
  11.5 32.0 %collective-permute-start.7 = (bf16[256,2048]{1,0:T(8,128)(2,1)}, bf16[256,2048]{1,0:T(8,128)(2,1)}, u32[]{:S(2)}, u32[]{:S(2)}) collective-permute-start(bf16[256,2048]{1,0:T(8,128)(2,1)} %get-tuple-element.22), channel_id=1, source_target_pairs={{4,0},{8,4},{12,8},{14,12},{10,14},{6,10},{2,6},{0,2},{5,1},{9,5},... | collective-permute-start | bytes 3145736 | tf_op jit(solution)/shard_map/ppermute | solution.py:114
  24.8 101.0 %collective-permute-start.22 = (bf16[1024,1024]{1,0:T(8,128)(2,1)S(1)}, bf16[1024,1024]{1,0:T(8,128)(2,1)S(1)}, u32[]{:S(2)}, u32[]{:S(2)}) collective-permute-start(bf16[1024,1024]{1,0:T(8,128)(2,1)S(1)} %copy-done.5), channel_id=1, source_target_pairs={{0,1},{1,0},{2,3},{3,2},{4,5},{5,4},{6,7},{7,6},{8,9},{9,8},{10,11... | collective-permute-start | bytes 6291464 | tf_op jit(solution)/shard_map/ppermute | solution.py:127
  26.0 26.4 %collective-permute-start.29 = (bf16[1024,256]{1,0:T(8,128)(2,1)}, bf16[1024,256]{1,0:T(8,128)(2,1)S(1)}, u32[]{:S(2)}, u32[]{:S(2)}) collective-permute-start(bf16[1024,256]{1,0:T(8,128)(2,1)} %collective-permute-done.27), channel_id=1, source_target_pairs={{0,4},{4,8},{8,12},{12,14},{14,10},{10,6},{6,2},{2,0},{1,5},{5,9},... | collective-permute-start | bytes 1572872 | tf_op jit(solution)/shard_map/ppermute | solution.py:113
  29.2 28.7 %collective-permute-start.30 = (bf16[1024,256]{1,0:T(8,128)(2,1)}, bf16[1024,256]{1,0:T(8,128)(2,1)S(1)}, u32[]{:S(2)}, u32[]{:S(2)}) collective-permute-start(bf16[1024,256]{1,0:T(8,128)(2,1)} %collective-permute-done.28), channel_id=1, source_target_pairs={{4,0},{8,4},{12,8},{14,12},{10,14},{6,10},{2,6},{0,2},{5,1},{9,5},... | collective-permute-start | bytes 1572872 | tf_op jit(solution)/shard_map/ppermute | solution.py:114
  39.3 46.5 %collective-permute-start.3 = (bf16[128,512]{1,0:T(8,128)(2,1)S(1)}, bf16[128,512]{1,0:T(8,128)(2,1)S(1)}, u32[]{:S(2)}, u32[]{:S(2)}) collective-permute-start(bf16[128,512]{1,0:T(8,128)(2,1)S(1)} %dynamic-slice_convert_fusion), channel_id=1, source_target_pairs={{4,0},{8,4},{12,8},{14,12},{10,14},{6,10},{2,6},{0,2},{5,1},{9,5},... | collective-permute-start | bytes 393224 | tf_op jit(solution)/shard_map/ppermute | solution.py:163
  52.5 33.5 %collective-permute-start.1 = (bf16[128,512]{1,0:T(8,128)(2,1)S(1)}, bf16[128,512]{1,0:T(8,128)(2,1)S(1)}, u32[]{:S(2)}, u32[]{:S(2)}) collective-permute-start(bf16[128,512]{1,0:T(8,128)(2,1)S(1)} %dynamic-slice_convert_fusion.1), channel_id=1, source_target_pairs={{0,4},{4,8},{8,12},{12,14},{14,10},{10,6},{6,2},{2,0},{1,5},{5,9},... | collective-permute-start | bytes 393224 | tf_op jit(solution)/shard_map/ppermute | solution.py:162
  56.1 71.9 %collective-permute-start.6 = (bf16[256,2048]{1,0:T(8,128)(2,1)}, bf16[256,2048]{1,0:T(8,128)(2,1)S(1)}, u32[]{:S(2)}, u32[]{:S(2)}) collective-permute-start(bf16[256,2048]{1,0:T(8,128)(2,1)} %collective-permute-done.5), channel_id=1, source_target_pairs={{0,4},{4,8},{8,12},{12,14},{14,10},{10,6},{6,2},{2,0},{1,5},{5,9},... | collective-permute-start | bytes 3145736 | tf_op jit(solution)/shard_map/ppermute | solution.py:113
  57.9 22.0 %collective-permute-start.16 = (f32[1024]{0:T(1024)S(1)}, f32[1024]{0:T(1024)S(1)}, u32[]{:S(2)}, u32[]{:S(2)}) collective-permute-start(f32[1024]{0:T(1024)S(1)} %add.73), channel_id=1, source_target_pairs={{0,8},{2,10},{4,12},{6,14},{8,0},{10,2},{12,4},{14,6},{1,9},{3,11}... | collective-permute-start | bytes 12296 | tf_op jit(solution)/shard_map/ppermute | solution.py:145
  79.9 21.3 %collective-permute-start.31 = (bf16[1024,256]{1,0:T(8,128)(2,1)S(1)}, bf16[1024,256]{1,0:T(8,128)(2,1)S(1)}, u32[]{:S(2)}, u32[]{:S(2)}) collective-permute-start(bf16[1024,256]{1,0:T(8,128)(2,1)S(1)} %collective-permute-done.29), channel_id=1, source_target_pairs={{0,4},{4,8},{8,12},{12,14},{14,10},{10,6},{6,2},{2,0},{1,5},{5,9},... | collective-permute-start | bytes 1572872 | tf_op jit(solution)/shard_map/ppermute | solution.py:113
  85.9 15.5 %collective-permute-start.32 = (bf16[1024,256]{1,0:T(8,128)(2,1)S(1)}, bf16[1024,256]{1,0:T(8,128)(2,1)S(1)}, u32[]{:S(2)}, u32[]{:S(2)}) collective-permute-start(bf16[1024,256]{1,0:T(8,128)(2,1)S(1)} %collective-permute-done.30), channel_id=1, source_target_pairs={{4,0},{8,4},{12,8},{14,12},{10,14},{6,10},{2,6},{0,2},{5,1},{9,5},... | collective-permute-start | bytes 1572872 | tf_op jit(solution)/shard_map/ppermute | solution.py:114
  85.9 12.9 %collective-permute-start.4 = (bf16[128,512]{1,0:T(8,128)(2,1)S(1)}, bf16[128,512]{1,0:T(8,128)(2,1)S(1)}, u32[]{:S(2)}, u32[]{:S(2)}) collective-permute-start(bf16[128,512]{1,0:T(8,128)(2,1)S(1)} %add_convert_fusion.10), channel_id=1, source_target_pairs={{4,0},{8,4},{12,8},{14,12},{10,14},{6,10},{2,6},{0,2},{5,1},{9,5},... | collective-permute-start | bytes 393224 | tf_op jit(solution)/shard_map/ppermute | solution.py:163
  101.2 26.9 %collective-permute-start.8 = (bf16[256,2048]{1,0:T(8,128)(2,1)}, bf16[256,2048]{1,0:T(8,128)(2,1)S(1)}, u32[]{:S(2)}, u32[]{:S(2)}) collective-permute-start(bf16[256,2048]{1,0:T(8,128)(2,1)} %collective-permute-done.7), channel_id=1, source_target_pairs={{4,0},{8,4},{12,8},{14,12},{10,14},{6,10},{2,6},{0,2},{5,1},{9,5},... | collective-permute-start | bytes 3145736 | tf_op jit(solution)/shard_map/ppermute | solution.py:114
  104.3 21.4 %collective-permute-start.34 = (bf16[512,256]{1,0:T(8,128)(2,1)S(1)}, bf16[512,256]{1,0:T(8,128)(2,1)S(1)}, u32[]{:S(2)}, u32[]{:S(2)}) collective-permute-start(bf16[512,256]{1,0:T(8,128)(2,1)S(1)} %slice.88), channel_id=1, source_target_pairs={{4,0},{8,4},{12,8},{14,12},{10,14},{6,10},{2,6},{0,2},{5,1},{9,5},... | collective-permute-start | bytes 786440 | tf_op jit(solution)/shard_map/ppermute | solution.py:120
  130.2 38.7 %collective-permute-start.23 = (bf16[256,2048]{1,0:T(8,128)(2,1)S(1)}, bf16[256,2048]{1,0:T(8,128)(2,1)S(1)}, u32[]{:S(2)}, u32[]{:S(2)}) collective-permute-start(bf16[256,2048]{1,0:T(8,128)(2,1)S(1)} %collective-permute-done.6), channel_id=1, source_target_pairs={{0,4},{4,8},{8,12},{12,14},{14,10},{10,6},{6,2},{2,0},{1,5},{5,9},... | collective-permute-start | bytes 3145736 | tf_op jit(solution)/shard_map/ppermute | solution.py:113
  132.6 38.3 %collective-permute-start.24 = (bf16[256,2048]{1,0:T(8,128)(2,1)S(1)}, bf16[256,2048]{1,0:T(8,128)(2,1)S(1)}, u32[]{:S(2)}, u32[]{:S(2)}) collective-permute-start(bf16[256,2048]{1,0:T(8,128)(2,1)S(1)} %collective-permute-done.8), channel_id=1, source_target_pairs={{4,0},{8,4},{12,8},{14,12},{10,14},{6,10},{2,6},{0,2},{5,1},{9,5},... | collective-permute-start | bytes 3145736 | tf_op jit(solution)/shard_map/ppermute | solution.py:114
  135.5 18.0 %collective-permute-start.10 = (bf16[128,512]{1,0:T(8,128)(2,1)S(1)}, bf16[128,512]{1,0:T(8,128)(2,1)S(1)}, u32[]{:S(2)}, u32[]{:S(2)}) collective-permute-start(bf16[128,512]{1,0:T(8,128)(2,1)S(1)} %add_convert_fusion.9), channel_id=1, source_target_pairs={{0,4},{4,8},{8,12},{12,14},{14,10},{10,6},{6,2},{2,0},{1,5},{5,9},... | collective-permute-start | bytes 393224 | tf_op jit(solution)/shard_map/ppermute | solution.py:162
  137.6 18.5 %collective-permute-start.18 = (bf16[128,512]{1,0:T(8,128)(2,1)S(1)}, bf16[128,512]{1,0:T(8,128)(2,1)S(1)}, u32[]{:S(2)}, u32[]{:S(2)}) collective-permute-start(bf16[128,512]{1,0:T(8,128)(2,1)S(1)} %add_convert_fusion.5), channel_id=1, source_target_pairs={{4,0},{8,4},{12,8},{14,12},{10,14},{6,10},{2,6},{0,2},{5,1},{9,5},... | collective-permute-start | bytes 393224 | tf_op jit(solution)/shard_map/ppermute | solution.py:163
  166.5 15.1 %collective-permute-start.13 = (bf16[128,512]{1,0:T(8,128)(2,1)S(1)}, bf16[128,512]{1,0:T(8,128)(2,1)S(1)}, u32[]{:S(2)}, u32[]{:S(2)}) collective-permute-start(bf16[128,512]{1,0:T(8,128)(2,1)S(1)} %add_convert_fusion.6), channel_id=1, source_target_pairs={{0,4},{4,8},{8,12},{12,14},{14,10},{10,6},{6,2},{2,0},{1,5},{5,9},... | collective-permute-start | bytes 393224 | tf_op jit(solution)/shard_map/ppermute | solution.py:162
  168.7 12.9 %collective-permute-start.21 = (bf16[128,512]{1,0:T(8,128)(2,1)S(1)}, bf16[128,512]{1,0:T(8,128)(2,1)S(1)}, u32[]{:S(2)}, u32[]{:S(2)}) collective-permute-start(bf16[128,512]{1,0:T(8,128)(2,1)S(1)} %add_convert_fusion.2), channel_id=1, source_target_pairs={{4,0},{8,4},{12,8},{14,12},{10,14},{6,10},{2,6},{0,2},{5,1},{9,5},... | collective-permute-start | bytes 393224 | tf_op jit(solution)/shard_map/ppermute | solution.py:163
  169.0 12.8 %collective-permute-start.25 = (bf16[128,2048]{1,0:T(8,128)(2,1)S(1)}, bf16[128,2048]{1,0:T(8,128)(2,1)S(1)}, u32[]{:S(2)}, u32[]{:S(2)}) collective-permute-start(bf16[128,2048]{1,0:T(8,128)(2,1)S(1)} %slice.82), channel_id=1, source_target_pairs={{0,4},{4,8},{8,12},{12,14},{14,10},{10,6},{6,2},{2,0},{1,5},{5,9},... | collective-permute-start | bytes 1572872 | tf_op jit(solution)/shard_map/ppermute | solution.py:119
  (22 other events, 253.6 us)

commit v3 on v2

--- a/solution.py
+++ b/solution.py
@@ -106,10 +106,14 @@
         sizes = (size, array.shape[1]) if axis == 0 else (array.shape[0], size)
         return lax.dynamic_slice(array, begin, sizes)
 
-    def gather(block):
+    def gather(block, gate=None):
         got = []
         ahead_block = back_block = block
         for step in range(1, count // 2):
+            if step == 3 and gate is not None:
+                ahead_block, back_block, gate = lax.optimization_barrier(
+                    (ahead_block, back_block, gate)
+                )
             ahead_block = lax.ppermute(ahead_block, "row", ahead)
             back_block = lax.ppermute(back_block, "row", back)
             got.append((row_at(-step), ahead_block, row_at(step), back_block))
@@ -121,7 +125,7 @@
             ],
             axis=0,
         )
-        return got, (row_at(count // 2), last)
+        return got, (row_at(count // 2), last), gate
 
     def both(block, axis):
         other = lax.ppermute(block, "col", swap)
@@ -130,20 +134,11 @@
         return jnp.concatenate([low, high], axis=axis)
 
     joined = jnp.concatenate([expert_query, expert_key, expert_value], axis=1)
-    weight_pairs, weight_last = gather(joined)
-
     states = both(prefix_states, 0)
+    states, action_states = lax.optimization_barrier((states, action_states))
     wide = states.astype(F32)
     squares = jnp.sum(wide * wide, axis=1)
     features = prefix_states.shape[1] * count
-    if count & (count - 1):
-        squares = lax.psum(squares, "row")
-    else:
-        hop = 1
-        while hop < count:
-            pairs = [(r, r ^ hop) for r in range(count)]
-            squares += lax.ppermute(squares, "row", pairs)
-            hop *= 2
     scaled = (wide * prefix_gain[None, :]).astype(BF16)
     key_part = jnp.dot(scaled, backbone_key, preferred_element_type=F32)
     value_part = jnp.dot(scaled, backbone_value, preferred_element_type=F32)
@@ -154,13 +149,17 @@
 
     key_run = part(key_part, row_at(-1))
     value_run = part(value_part, row_at(1))
+    doubling = count & (count - 1) == 0
+    if not doubling:
+        squares = lax.psum(squares, "row")
     for step in range(count - 1):
-        if step == 2 and len(weight_pairs) > 2:
-            key_run, value_run, _, _ = lax.optimization_barrier(
-                (key_run, value_run, weight_pairs[1][1], weight_pairs[1][3])
-            )
-        key_run = lax.ppermute(key_run.astype(BF16), "row", ahead).astype(F32)
-        value_run = lax.ppermute(value_run.astype(BF16), "row", back).astype(F32)
+        key_run, value_run = key_run.astype(BF16), value_run.astype(BF16)
+        if doubling and 1 << step < count:
+            key_run, value_run, squares = lax.optimization_barrier((key_run, value_run, squares))
+            pairs = [(r, r ^ (1 << step)) for r in range(count)]
+            squares += lax.ppermute(squares, "row", pairs)
+        key_run = lax.ppermute(key_run, "row", ahead).astype(F32)
+        value_run = lax.ppermute(value_run, "row", back).astype(F32)
         key_run += part(key_part, row_at(-2 - step))
         value_run += part(value_part, row_at(2 + step - count))
     own_squares = lax.dynamic_slice(squares, (mine * own,), (own,))
@@ -168,7 +167,9 @@
     prefix_keys = (key_run * row_scale).astype(BF16)
     prefix_values = (value_run * row_scale).astype(BF16)
 
-    action_states, states = lax.optimization_barrier((action_states, states))
+    weight_pairs, weight_last, (prefix_keys, prefix_values) = gather(
+        joined, (prefix_keys, prefix_values)
+    )
     actions = both(action_states, 1)
     depth = joined.shape[0]
 
@@ -176,6 +177,7 @@
         return cut(actions, row * depth, depth, 1)
 
     row_c, block_c = weight_last
+    later, block_c = lax.optimization_barrier((expert_out, block_c))
     blocks = [(mine, joined)]
     for row_a, block_a, row_b, block_b in weight_pairs:
         blocks += [(row_a, block_a), (row_b, block_b)]
@@ -196,8 +198,7 @@
     action_key = projected[:, query_cols : query_cols + key_cols]
     action_value = projected[:, query_cols + key_cols :]
 
-    later, _ = lax.optimization_barrier((expert_out, block_c))
-    out_pairs, out_last = gather(later)
+    out_pairs, out_last, _ = gather(later)
     piece = expert_out.shape[1]
     out_weight = jnp.zeros((expert_out.shape[0], piece * count), BF16)
     placed = [(mine, expert_out)]

time: 222 us -> 240 us (1.081)
  local copies, waits for them, and re-layouts: 17.9 us -> 29.1 us
  other arithmetic: 9.11 us -> 20 us
  starting transfers between devices: 47.5 us -> 38.5 us
  waiting for transfers between devices: 87.1 us -> 90.1 us
    ppermute x14, waiting for transfers between devices: 35.6 us -> 79 us  [the longest x7 45.3 us: shards(): value_run = lax.ppermute(value_run, 'row', back).astype(F32)]
    ppermute x3, waiting for transfers between devices: 24.6 us -> 0.61 us  [shards(): squares += lax.ppermute(squares, 'row', pairs)]
    ppermute x2, waiting for transfers between devices: 17.6 us -> 0.4 us  [gather(): lax.ppermute(back_block[half:], 'row', back)]
    ppermute x6, starting transfers between devices: 16.7 us -> 5.97 us  [gather(): ahead_block = lax.ppermute(ahead_block, 'row', ahead)]
    convert_element_type x10 -> x13, other arithmetic: 0.34 us -> 7.6 us  [the longest x1 7.21 us: shards(): projected = total.astype(BF16)]
    ppermute x6, starting transfers between devices: 0.19 us -> 6.34 us  [gather(): back_block = lax.ppermute(back_block, 'row', back)]
    dynamic_update_slice x7, local copies, waits for them, and re-layouts: 2.52 us -> 8.15 us  [shards(): lax.dynamic_update_slice(out_weight, block, (zero, row * piece))]
    ppermute x3, starting transfers between devices: 7.51 us -> 3.48 us  [shards(): squares += lax.ppermute(squares, 'row', pairs)]
  transfers between devices with their start and end apart: 36 -> 36, of which waited for: 13 -> 18; matrix products, arithmetic and copies ran while one was open for 18% -> 25% of each run, Pallas kernels for 0% -> 9%
where the time goes in v3:
time: 240 us; the launch traced here: 239 us
  waiting for transfers between devices  90.1 us (38%)
  starting transfers between devices  38.5 us (16%)
  local copies, waits for them, and re-layouts  29.1 us (12%)
  matrix products  27.9 us (12%)
  Pallas kernels  21.3 us (9%)
  other arithmetic  20 us (8%)
  between operations  12.4 us (5%)
    ppermute x7, waiting for transfers between devices, shards(): value_run = lax.ppermute(value_run, 'row', back).astype(F32)  45.3 us
    ppermute x7, waiting for transfers between devices, shards(): key_run = lax.ppermute(key_run, 'row', ahead).astype(F32)  33.7 us
    pallas_call x1, Pallas kernels, attend(): pl.pallas_call(functools.partial(attend_kernel, HEAD ** (-0.5) * math.log...  21.3 us
    dot_general x2, matrix products, product_of(): jnp.dot(jnp.concatenate([columns(row) for row, _ in some], axis=1), jnp.c...  16.1 us
    unnamed x44, local copies, waits for them, and re-layouts  12.1 us
    ppermute x7, starting transfers between devices, shards(): key_run = lax.ppermute(key_run, 'row', ahead).astype(F32)  11.9 us
    dot_general x2, matrix products, product(): return jnp.dot(attended, weight, preferred_element_type=F32)  9.25 us
    dynamic_update_slice x7, local copies, waits for them, and re-layouts, shards(): lax.dynamic_update_slice(out_weight, block, (zero, row * piece))  8.15 us
  transfers between devices with their start and end apart: 36, of which 18 were waited for; matrix products, arithmetic and copies ran while one was open for 25% of the time, Pallas kernels for 9%

profile of v3, /device:TPU:0, one launch (start us, length us, event | category | flops | bytes accessed | tf_op | source)
XLA Modules:
  0.0 239.3 jit_solution(9213729609450706050)
XLA Ops:
  10.6 2.7 %collective-permute-start.5 = (bf16[128,512]{1,0:T(8,128)(2,1)S(1)}, bf16[128,512]{1,0:T(8,128)(2,1)S(1)}, u32[]{:S(2)}, u32[]{:S(2)}) collective-permute-start(bf16[128,512]{1,0:T(8,128)(2,1)S(1)} %get-tuple-element.21), channel_id=1, source_target_pairs={{0,4},{4,8},{8,12},{12,14},{14,10},{10,6},{6,2},{2,0},{1,5},{5,9},... | collective-permute-start | bytes 393224 | tf_op jit(solution)/shard_map/ppermute | solution.py:161
  20.3 24.0 %collective-permute-done.6 = bf16[128,512]{1,0:T(8,128)(2,1)S(1)} collective-permute-done((bf16[128,512]{1,0:T(8,128)(2,1)S(1)}, bf16[128,512]{1,0:T(8,128)(2,1)S(1)}, u32[]{:S(2)}, u32[]{:S(2)}) %collective-permute-start.6) | collective-permute-done | bytes 131104 | tf_op jit(solution)/shard_map/ppermute | solution.py:162
  49.6 4.5 %collective-permute-done.9 = bf16[128,512]{1,0:T(8,128)(2,1)S(1)} collective-permute-done((bf16[128,512]{1,0:T(8,128)(2,1)S(1)}, bf16[128,512]{1,0:T(8,128)(2,1)S(1)}, u32[]{:S(2)}, u32[]{:S(2)}) %collective-permute-start.9) | collective-permute-done | bytes 131104 | tf_op jit(solution)/shard_map/ppermute | solution.py:162
  60.6 23.0 %collective-permute-done.11 = bf16[128,512]{1,0:T(8,128)(2,1)S(1)} collective-permute-done((bf16[128,512]{1,0:T(8,128)(2,1)S(1)}, bf16[128,512]{1,0:T(8,128)(2,1)S(1)}, u32[]{:S(2)}, u32[]{:S(2)}) %collective-permute-start.11) | collective-permute-done | bytes 131104 | tf_op jit(solution)/shard_map/ppermute | solution.py:161
  84.5 4.4 %collective-permute-done.18 = bf16[128,512]{1,0:T(8,128)(2,1)S(1)} collective-permute-done((bf16[128,512]{1,0:T(8,128)(2,1)S(1)}, bf16[128,512]{1,0:T(8,128)(2,1)S(1)}, u32[]{:S(2)}, u32[]{:S(2)}) %collective-permute-start.18) | collective-permute-done | bytes 131104 | tf_op jit(solution)/shard_map/ppermute | solution.py:162
  90.7 3.2 %collective-permute-done.12 = bf16[128,512]{1,0:T(8,128)(2,1)S(1)} collective-permute-done((bf16[128,512]{1,0:T(8,128)(2,1)S(1)}, bf16[128,512]{1,0:T(8,128)(2,1)S(1)}, u32[]{:S(2)}, u32[]{:S(2)}) %collective-permute-start.12) | collective-permute-done | bytes 131104 | tf_op jit(solution)/shard_map/ppermute | solution.py:161
  94.6 4.3 %collective-permute-done.19 = bf16[128,512]{1,0:T(8,128)(2,1)S(1)} collective-permute-done((bf16[128,512]{1,0:T(8,128)(2,1)S(1)}, bf16[128,512]{1,0:T(8,128)(2,1)S(1)}, u32[]{:S(2)}, u32[]{:S(2)}) %collective-permute-start.19) | collective-permute-done | bytes 131104 | tf_op jit(solution)/shard_map/ppermute | solution.py:162
  100.7 3.2 %collective-permute-done.13 = bf16[128,512]{1,0:T(8,128)(2,1)S(1)} collective-permute-done((bf16[128,512]{1,0:T(8,128)(2,1)S(1)}, bf16[128,512]{1,0:T(8,128)(2,1)S(1)}, u32[]{:S(2)}, u32[]{:S(2)}) %collective-permute-start.13) | collective-permute-done | bytes 131104 | tf_op jit(solution)/shard_map/ppermute | solution.py:161
  104.5 4.3 %collective-permute-done.20 = bf16[128,512]{1,0:T(8,128)(2,1)S(1)} collective-permute-done((bf16[128,512]{1,0:T(8,128)(2,1)S(1)}, bf16[128,512]{1,0:T(8,128)(2,1)S(1)}, u32[]{:S(2)}, u32[]{:S(2)}) %collective-permute-start.20) | collective-permute-done | bytes 131104 | tf_op jit(solution)/shard_map/ppermute | solution.py:162
  110.6 3.2 %collective-permute-done.14 = bf16[128,512]{1,0:T(8,128)(2,1)S(1)} collective-permute-done((bf16[128,512]{1,0:T(8,128)(2,1)S(1)}, bf16[128,512]{1,0:T(8,128)(2,1)S(1)}, u32[]{:S(2)}, u32[]{:S(2)}) %collective-permute-start.14) | collective-permute-done | bytes 131104 | tf_op jit(solution)/shard_map/ppermute | solution.py:161
  116.7 3.5 %collective-permute-done.21 = bf16[128,512]{1,0:T(8,128)(2,1)S(1)} collective-permute-done((bf16[128,512]{1,0:T(8,128)(2,1)S(1)}, bf16[128,512]{1,0:T(8,128)(2,1)S(1)}, u32[]{:S(2)}, u32[]{:S(2)}) %collective-permute-start.21) | collective-permute-done | bytes 131104 | tf_op jit(solution)/shard_map/ppermute | solution.py:162
  124.6 2.5 %broadcast_in_dim.2 = bf16[1024,2048]{1,0:T(8,128)(2,1)} broadcast(bf16[]{:T(256)} %constant.42.clone.1), dimensions={} | broadcast | bytes 4194306 | tf_op jit(solution)/shard_map/broadcast_in_dim | solution.py:203
  134.0 2.3 constant_dynamic-update-slice_fusion.6
  136.3 2.3 constant_dynamic-update-slice_fusion.5
  140.9 2.3 constant_dynamic-update-slice_fusion.3
  153.8 7.8 %fusion.42 = f32[1024,2048]{1,0:T(8,128)} fusion(bf16[1024,1280]{1,0:T(8,128)(2,1)S(1)} %fusion.36, bf16[1280,2048]{1,0:T(8,128)(2,1)S(1)} %bitcast.22), kind=kOutput, calls=%fused_computation.100 | convolution fusion | flops 5368709120 | bytes 16252928 | tf_op jit(solution)/shard_map/dot_general | solution.py:188
  163.8 8.3 %fusion.2 = f32[1024,2048]{1,0:T(8,128)} fusion(bf16[256,2048]{1,0:T(8,128)(2,1)S(1)} %pad_maximum_fusion.1, bf16[256,2048]{1,0:T(8,128)(2,1)} %collective-permute-done.24, bf16[256,2048]{1,0:T(8,128)(2,1)} %collective-permute-done.23, bf16[1024,256]{1,0:T(8,128)(2,1)S(1)} %get-tuple-element.42, bf16[1024,256]{1,0:T(8,128)(2,1)S(1)} %get-tuple-element.41, ...), kind=kOutput, calls=%fused_computation.22 | convolution fusion | flops 3235381248 | bytes 13107200 | tf_op jit(solution)/shard_map/dot_general | solution.py:188
  172.1 3.8 %collective-permute-done.27 = bf16[1024,256]{1,0:T(8,128)(2,1)S(1)} collective-permute-done((bf16[1024,256]{1,0:T(8,128)(2,1)S(1)}, bf16[1024,256]{1,0:T(8,128)(2,1)S(1)}, u32[]{:S(2)}, u32[]{:S(2)}) %collective-permute-start.27) | collective-permute-done | bytes 524320 | tf_op jit(solution)/shard_map/ppermute | solution.py:117
  178.0 7.2 %add_convert_fusion = bf16[1024,2048]{1,0:T(8,128)(2,1)S(1)} fusion(f32[1024,2048]{1,0:T(8,128)} %fusion.42, f32[1024,2048]{1,0:T(8,128)} %fusion.2), kind=kLoop, calls=%fused_computation | loop fusion | flops 4194304 | bytes 20971520 | tf_op jit(solution)/shard_map/convert_element_type | solution.py:195
  185.6 4.0 %collective-permute-done.29 = bf16[1024,256]{1,0:T(8,128)(2,1)} collective-permute-done((bf16[1024,256]{1,0:T(8,128)(2,1)S(1)}, bf16[1024,256]{1,0:T(8,128)(2,1)}, u32[]{:S(2)}, u32[]{:S(2)}) %collective-permute-start.29) | collective-permute-done | bytes 524320 | tf_op jit(solution)/shard_map/ppermute | solution.py:117
  191.6 21.3 %attend.1 = bf16[1024,1024]{1,0:T(8,128)(2,1)S(1)} custom-call(s32[1]{0:T(128)S(6)} %copy.35.plen_ref, s32[1]{0:T(128)S(6)} %copy.36.alen_ref, bf16[1024,1024]{1,0:T(8,128)(2,1)S(1)} %slice.84.q_ref, bf16[128,512]{1,0:T(8,128)(2,1)S(1)} %get-tuple-element.17.pk_ref, bf16[1024,512]{1,0:T(8,128)(2,1)S(1)} %get-tuple-element.38.ak_ref, ...), custom_call_target="tpu_custom_call" | custom-call | flops 9663676416 | bytes 4194304 | tf_op jit(solution)/shard_map/attend/pallas_call | solution.py:49
  225.7 5.2 %fusion.12 = bf16[1024,1024]{1,0:T(8,128)(2,1)} fusion(bf16[1024,1024]{1,0:T(8,128)(2,1)S(1)} %attend.1, bf16[1024,2048]{1,0:T(8,128)(2,1)} %maximum_dynamic-update-slice_fusion, u32[]{:T(128)S(6)} %mul.182), kind=kOutput, calls=%fused_computation.35 | convolution fusion | flops 2148532224 | bytes 6291460 | tf_op jit(solution)/shard_map/dot_general | solution.py:218
  231.0 4.0 %fusion.10 = f32[1024,1024]{1,0:T(8,128)S(1)} fusion(bf16[1024,1024]{1,0:T(8,128)(2,1)S(1)} %attend.1, bf16[1024,2048]{1,0:T(8,128)(2,1)} %maximum_dynamic-update-slice_fusion, u32[]{:T(128)S(6)} %mul.181), kind=kOutput, calls=%fused_computation.31 | convolution fusion | flops 2147483648 | bytes 8388612 | tf_op jit(solution)/shard_map/dot_general | solution.py:218
  235.5 3.8 %add_convert_fusion.1 = bf16[1024,1024]{1,0:T(8,128)(2,1)} fusion(f32[1024,1024]{1,0:T(8,128)S(1)} %fusion.10, bf16[1024,1024]{1,0:T(8,128)(2,1)} %collective-permute-done.35), kind=kLoop, calls=%fused_computation.21 | loop fusion | flops 3145728 | bytes 8388608 | tf_op jit(solution)/shard_map/convert_element_type | solution.py:223
  (148 shorter events, 71.6 us)
Async XLA Ops:
  10.6 9.7 %collective-permute-start.5 = (bf16[128,512]{1,0:T(8,128)(2,1)S(1)}, bf16[128,512]{1,0:T(8,128)(2,1)S(1)}, u32[]{:S(2)}, u32[]{:S(2)}) collective-permute-start(bf16[128,512]{1,0:T(8,128)(2,1)S(1)} %get-tuple-element.21), channel_id=1, source_target_pairs={{0,4},{4,8},{8,12},{12,14},{14,10},{10,6},{6,2},{2,0},{1,5},{5,9},... | collective-permute-start | bytes 393224 | tf_op jit(solution)/shard_map/ppermute | solution.py:161
  14.1 6.2 %collective-permute-start.7 = (f32[1024]{0:T(1024)S(1)}, f32[1024]{0:T(1024)S(1)}, u32[]{:S(2)}, u32[]{:S(2)}) collective-permute-start(f32[1024]{0:T(1024)S(1)} %fusion.1), channel_id=1, source_target_pairs={{0,2},{2,0},{4,6},{6,4},{8,10},{10,8},{12,14},{14,12},{1,3},{3,1},... | collective-permute-start | bytes 12296 | tf_op jit(solution)/shard_map/ppermute | solution.py:160
  14.9 40.1 %collective-permute-start = (bf16[256,2048]{1,0:T(8,128)(2,1)S(1)}, bf16[256,2048]{1,0:T(8,128)(2,1)}, u32[]{:S(2)}, u32[]{:S(2)}) collective-permute-start(bf16[256,2048]{1,0:T(8,128)(2,1)S(1)} %get-tuple-element.50), channel_id=1, source_target_pairs={{0,4},{4,8},{8,12},{12,14},{14,10},{10,6},{6,2},{2,0},{1,5},{5,9},... | collective-permute-start | bytes 3145736 | tf_op jit(solution)/shard_map/ppermute | solution.py:117
  16.8 40.2 %collective-permute-start.2 = (bf16[256,2048]{1,0:T(8,128)(2,1)S(1)}, bf16[256,2048]{1,0:T(8,128)(2,1)}, u32[]{:S(2)}, u32[]{:S(2)}) collective-permute-start(bf16[256,2048]{1,0:T(8,128)(2,1)S(1)} %get-tuple-element.50), channel_id=1, source_target_pairs={{4,0},{8,4},{12,8},{14,12},{10,14},{6,10},{2,6},{0,2},{5,1},{9,5},... | collective-permute-start | bytes 3145736 | tf_op jit(solution)/shard_map/ppermute | solution.py:118
  18.2 26.1 %collective-permute-start.6 = (bf16[128,512]{1,0:T(8,128)(2,1)S(1)}, bf16[128,512]{1,0:T(8,128)(2,1)S(1)}, u32[]{:S(2)}, u32[]{:S(2)}) collective-permute-start(bf16[128,512]{1,0:T(8,128)(2,1)S(1)} %get-tuple-element.22), channel_id=1, source_target_pairs={{4,0},{8,4},{12,8},{14,12},{10,14},{6,10},{2,6},{0,2},{5,1},{9,5},... | collective-permute-start | bytes 393224 | tf_op jit(solution)/shard_map/ppermute | solution.py:162
  54.9 92.9 %collective-permute-start.22 = (bf16[1024,1024]{1,0:T(8,128)(2,1)S(1)}, bf16[1024,1024]{1,0:T(8,128)(2,1)}, u32[]{:S(2)}, u32[]{:S(2)}) collective-permute-start(bf16[1024,1024]{1,0:T(8,128)(2,1)S(1)} %copy-done.4), channel_id=1, source_target_pairs={{0,1},{1,0},{2,3},{3,2},{4,5},{5,4},{6,7},{7,6},{8,9},{9,8},{10,11... | collective-permute-start | bytes 6291464 | tf_op jit(solution)/shard_map/ppermute | solution.py:131
  55.0 67.6 %collective-permute-start.1 = (bf16[256,2048]{1,0:T(8,128)(2,1)}, bf16[256,2048]{1,0:T(8,128)(2,1)}, u32[]{:S(2)}, u32[]{:S(2)}) collective-permute-start(bf16[256,2048]{1,0:T(8,128)(2,1)} %collective-permute-done), channel_id=1, source_target_pairs={{0,4},{4,8},{8,12},{12,14},{14,10},{10,6},{6,2},{2,0},{1,5},{5,9},... | collective-permute-start | bytes 3145736 | tf_op jit(solution)/shard_map/ppermute | solution.py:117
  57.0 65.5 %collective-permute-start.3 = (bf16[256,2048]{1,0:T(8,128)(2,1)}, bf16[256,2048]{1,0:T(8,128)(2,1)}, u32[]{:S(2)}, u32[]{:S(2)}) collective-permute-start(bf16[256,2048]{1,0:T(8,128)(2,1)} %collective-permute-done.2), channel_id=1, source_target_pairs={{4,0},{8,4},{12,8},{14,12},{10,14},{6,10},{2,6},{0,2},{5,1},{9,5},... | collective-permute-start | bytes 3145736 | tf_op jit(solution)/shard_map/ppermute | solution.py:118
  57.0 57.9 %collective-permute-start.16 = (f32[1024]{0:T(1024)S(1)}, f32[1024]{0:T(1024)S(1)}, u32[]{:S(2)}, u32[]{:S(2)}) collective-permute-start(f32[1024]{0:T(1024)S(1)} %add.68), channel_id=1, source_target_pairs={{0,8},{2,10},{4,12},{6,14},{8,0},{10,2},{12,4},{14,6},{1,9},{3,11}... | collective-permute-start | bytes 12296 | tf_op jit(solution)/shard_map/ppermute | solution.py:160
  59.2 24.3 %collective-permute-start.11 = (bf16[128,512]{1,0:T(8,128)(2,1)S(1)}, bf16[128,512]{1,0:T(8,128)(2,1)S(1)}, u32[]{:S(2)}, u32[]{:S(2)}) collective-permute-start(bf16[128,512]{1,0:T(8,128)(2,1)S(1)} %add_convert_fusion.11), channel_id=1, source_target_pairs={{0,4},{4,8},{8,12},{12,14},{14,10},{10,6},{6,2},{2,0},{1,5},{5,9},... | collective-permute-start | bytes 393224 | tf_op jit(solution)/shard_map/ppermute | solution.py:161
  113.8 6.4 %collective-permute-start.21 = (bf16[128,512]{1,0:T(8,128)(2,1)S(1)}, bf16[128,512]{1,0:T(8,128)(2,1)S(1)}, u32[]{:S(2)}, u32[]{:S(2)}) collective-permute-start(bf16[128,512]{1,0:T(8,128)(2,1)S(1)} %add_convert_fusion.2), channel_id=1, source_target_pairs={{4,0},{8,4},{12,8},{14,12},{10,14},{6,10},{2,6},{0,2},{5,1},{9,5},... | collective-permute-start | bytes 393224 | tf_op jit(solution)/shard_map/ppermute | solution.py:162
  115.0 6.4 %collective-permute-start.15 = (bf16[128,512]{1,0:T(8,128)(2,1)S(1)}, bf16[128,512]{1,0:T(8,128)(2,1)S(1)}, u32[]{:S(2)}, u32[]{:S(2)}) collective-permute-start(bf16[128,512]{1,0:T(8,128)(2,1)S(1)} %add_convert_fusion.6), channel_id=1, source_target_pairs={{0,4},{4,8},{8,12},{12,14},{14,10},{10,6},{6,2},{2,0},{1,5},{5,9},... | collective-permute-start | bytes 393224 | tf_op jit(solution)/shard_map/ppermute | solution.py:161
  122.5 20.7 %collective-permute-start.24 = (bf16[256,2048]{1,0:T(8,128)(2,1)}, bf16[256,2048]{1,0:T(8,128)(2,1)}, u32[]{:S(2)}, u32[]{:S(2)}) collective-permute-start(bf16[256,2048]{1,0:T(8,128)(2,1)} %collective-permute-done.3), channel_id=1, source_target_pairs={{4,0},{8,4},{12,8},{14,12},{10,14},{6,10},{2,6},{0,2},{5,1},{9,5},... | collective-permute-start | bytes 3145736 | tf_op jit(solution)/shard_map/ppermute | solution.py:118
  124.3 21.8 %collective-permute-start.23 = (bf16[256,2048]{1,0:T(8,128)(2,1)}, bf16[256,2048]{1,0:T(8,128)(2,1)}, u32[]{:S(2)}, u32[]{:S(2)}) collective-permute-start(bf16[256,2048]{1,0:T(8,128)(2,1)} %collective-permute-done.1), channel_id=1, source_target_pairs={{0,4},{4,8},{8,12},{12,14},{14,10},{10,6},{6,2},{2,0},{1,5},{5,9},... | collective-permute-start | bytes 3145736 | tf_op jit(solution)/shard_map/ppermute | solution.py:117
  144.4 17.3 %collective-permute-start.26 = (bf16[128,2048]{1,0:T(8,128)(2,1)S(1)}, bf16[128,2048]{1,0:T(8,128)(2,1)S(1)}, u32[]{:S(2)}, u32[]{:S(2)}) collective-permute-start(bf16[128,2048]{1,0:T(8,128)(2,1)S(1)} %slice.83), channel_id=1, source_target_pairs={{4,0},{8,4},{12,8},{14,12},{10,14},{6,10},{2,6},{0,2},{5,1},{9,5},... | collective-permute-start | bytes 1572872 | tf_op jit(solution)/shard_map/ppermute | solution.py:124
  147.3 14.4 %collective-permute-start.25 = (bf16[128,2048]{1,0:T(8,128)(2,1)S(1)}, bf16[128,2048]{1,0:T(8,128)(2,1)S(1)}, u32[]{:S(2)}, u32[]{:S(2)}) collective-permute-start(bf16[128,2048]{1,0:T(8,128)(2,1)S(1)} %slice.82), channel_id=1, source_target_pairs={{0,4},{4,8},{8,12},{12,14},{14,10},{10,6},{6,2},{2,0},{1,5},{5,9},... | collective-permute-start | bytes 1572872 | tf_op jit(solution)/shard_map/ppermute | solution.py:123
  161.8 14.2 %collective-permute-start.27 = (bf16[1024,256]{1,0:T(8,128)(2,1)S(1)}, bf16[1024,256]{1,0:T(8,128)(2,1)S(1)}, u32[]{:S(2)}, u32[]{:S(2)}) collective-permute-start(bf16[1024,256]{1,0:T(8,128)(2,1)S(1)} %copy-done.8), channel_id=1, source_target_pairs={{0,4},{4,8},{8,12},{12,14},{14,10},{10,6},{6,2},{2,0},{1,5},{5,9},... | collective-permute-start | bytes 1572872 | tf_op jit(solution)/shard_map/ppermute | solution.py:117
  162.8 13.5 %collective-permute-start.28 = (bf16[1024,256]{1,0:T(8,128)(2,1)S(1)}, bf16[1024,256]{1,0:T(8,128)(2,1)S(1)}, u32[]{:S(2)}, u32[]{:S(2)}) collective-permute-start(bf16[1024,256]{1,0:T(8,128)(2,1)S(1)} %copy-done.8), channel_id=1, source_target_pairs={{4,0},{8,4},{12,8},{14,12},{10,14},{6,10},{2,6},{0,2},{5,1},{9,5},... | collective-permute-start | bytes 1572872 | tf_op jit(solution)/shard_map/ppermute | solution.py:118
  175.9 13.6 %collective-permute-start.29 = (bf16[1024,256]{1,0:T(8,128)(2,1)S(1)}, bf16[1024,256]{1,0:T(8,128)(2,1)}, u32[]{:S(2)}, u32[]{:S(2)}) collective-permute-start(bf16[1024,256]{1,0:T(8,128)(2,1)S(1)} %collective-permute-done.27), channel_id=1, source_target_pairs={{0,4},{4,8},{8,12},{12,14},{14,10},{10,6},{6,2},{2,0},{1,5},{5,9},... | collective-permute-start | bytes 1572872 | tf_op jit(solution)/shard_map/ppermute | solution.py:117
  176.3 13.6 %collective-permute-start.30 = (bf16[1024,256]{1,0:T(8,128)(2,1)S(1)}, bf16[1024,256]{1,0:T(8,128)(2,1)}, u32[]{:S(2)}, u32[]{:S(2)}) collective-permute-start(bf16[1024,256]{1,0:T(8,128)(2,1)S(1)} %collective-permute-done.28), channel_id=1, source_target_pairs={{4,0},{8,4},{12,8},{14,12},{10,14},{6,10},{2,6},{0,2},{5,1},{9,5},... | collective-permute-start | bytes 1572872 | tf_op jit(solution)/shard_map/ppermute | solution.py:118
  189.6 28.6 %collective-permute-start.31 = (bf16[1024,256]{1,0:T(8,128)(2,1)}, bf16[1024,256]{1,0:T(8,128)(2,1)S(1)}, u32[]{:S(2)}, u32[]{:S(2)}) collective-permute-start(bf16[1024,256]{1,0:T(8,128)(2,1)} %collective-permute-done.29), channel_id=1, source_target_pairs={{0,4},{4,8},{8,12},{12,14},{14,10},{10,6},{6,2},{2,0},{1,5},{5,9},... | collective-permute-start | bytes 1572872 | tf_op jit(solution)/shard_map/ppermute | solution.py:117
  189.9 26.7 %collective-permute-start.32 = (bf16[1024,256]{1,0:T(8,128)(2,1)}, bf16[1024,256]{1,0:T(8,128)(2,1)S(1)}, u32[]{:S(2)}, u32[]{:S(2)}) collective-permute-start(bf16[1024,256]{1,0:T(8,128)(2,1)} %collective-permute-done.30), channel_id=1, source_target_pairs={{4,0},{8,4},{12,8},{14,12},{10,14},{6,10},{2,6},{0,2},{5,1},{9,5},... | collective-permute-start | bytes 1572872 | tf_op jit(solution)/shard_map/ppermute | solution.py:118
  216.6 6.4 %collective-permute-start.34 = (bf16[512,256]{1,0:T(8,128)(2,1)S(1)}, bf16[512,256]{1,0:T(8,128)(2,1)S(1)}, u32[]{:S(2)}, u32[]{:S(2)}) collective-permute-start(bf16[512,256]{1,0:T(8,128)(2,1)S(1)} %slice.88), channel_id=1, source_target_pairs={{4,0},{8,4},{12,8},{14,12},{10,14},{6,10},{2,6},{0,2},{5,1},{9,5},... | collective-permute-start | bytes 786440 | tf_op jit(solution)/shard_map/ppermute | solution.py:124
  218.2 6.6 %collective-permute-start.33 = (bf16[512,256]{1,0:T(8,128)(2,1)S(1)}, bf16[512,256]{1,0:T(8,128)(2,1)S(1)}, u32[]{:S(2)}, u32[]{:S(2)}) collective-permute-start(bf16[512,256]{1,0:T(8,128)(2,1)S(1)} %slice.87), channel_id=1, source_target_pairs={{0,4},{4,8},{8,12},{12,14},{14,10},{10,6},{6,2},{2,0},{1,5},{5,9},... | collective-permute-start | bytes 786440 | tf_op jit(solution)/shard_map/ppermute | solution.py:123
  (31 other events, 575.0 us)

commit v4 on v2

--- a/solution.py
+++ b/solution.py
@@ -130,45 +130,42 @@
         return jnp.concatenate([low, high], axis=axis)
 
     joined = jnp.concatenate([expert_query, expert_key, expert_value], axis=1)
-    weight_pairs, weight_last = gather(joined)
-
     states = both(prefix_states, 0)
+    states, action_states = lax.optimization_barrier((states, action_states))
     wide = states.astype(F32)
     squares = jnp.sum(wide * wide, axis=1)
     features = prefix_states.shape[1] * count
-    if count & (count - 1):
-        squares = lax.psum(squares, "row")
-    else:
-        hop = 1
-        while hop < count:
-            pairs = [(r, r ^ hop) for r in range(count)]
-            squares += lax.ppermute(squares, "row", pairs)
-            hop *= 2
     scaled = (wide * prefix_gain[None, :]).astype(BF16)
     key_part = jnp.dot(scaled, backbone_key, preferred_element_type=F32)
     value_part = jnp.dot(scaled, backbone_value, preferred_element_type=F32)
     own = states.shape[0] // count
 
-    def part(array, row):
-        return cut(array, row * own, own, 0)
-
-    key_run = part(key_part, row_at(-1))
-    value_run = part(value_part, row_at(1))
-    for step in range(count - 1):
-        if step == 2 and len(weight_pairs) > 2:
-            key_run, value_run, _, _ = lax.optimization_barrier(
-                (key_run, value_run, weight_pairs[1][1], weight_pairs[1][3])
-            )
-        key_run = lax.ppermute(key_run.astype(BF16), "row", ahead).astype(F32)
-        value_run = lax.ppermute(value_run.astype(BF16), "row", back).astype(F32)
-        key_run += part(key_part, row_at(-2 - step))
-        value_run += part(value_part, row_at(2 + step - count))
-    own_squares = lax.dynamic_slice(squares, (mine * own,), (own,))
-    row_scale = lax.rsqrt(own_squares / features + 1e-06)[:, None]
-    prefix_keys = (key_run * row_scale).astype(BF16)
-    prefix_values = (value_run * row_scale).astype(BF16)
-
-    action_states, states = lax.optimization_barrier((action_states, states))
+    high = lax.reduce_precision(squares, 8, 7)
+    middle = lax.reduce_precision(squares - high, 8, 7)
+    terms = jnp.stack([high, middle, squares - high - middle], axis=1)
+    terms = jnp.pad(terms, ((0, 0), (0, HEAD - terms.shape[1])))
+    share = jnp.concatenate([key_part, value_part, terms], axis=1)
+    outgoing = share.astype(BF16)
+    received = []
+    for step in range(1, count):
+        pairs = [(ring[p], ring[(p + step) % count]) for p in range(count)]
+        received.append(lax.ppermute(cut(outgoing, row_at(step) * own, own, 0), "row", pairs))
+
+    weight_pairs, weight_last = gather(joined)
+    if len(weight_pairs) > 1:
+        row_a, block_a, row_b, block_b = weight_pairs[1]
+        received, block_a, block_b = lax.optimization_barrier((received, block_a, block_b))
+        weight_pairs[1] = (row_a, block_a, row_b, block_b)
+    summed = cut(share, mine * own, own, 0)
+    for block in received:
+        summed += block.astype(F32)
+    key_cols = backbone_key.shape[1]
+    sums_end = 2 * key_cols
+    own_squares = jnp.sum(summed[:, sums_end : sums_end + 3], axis=1, keepdims=True)
+    row_scale = lax.rsqrt(own_squares / features + 1e-06)
+    prefix_keys = (summed[:, :key_cols] * row_scale).astype(BF16)
+    prefix_values = (summed[:, key_cols:sums_end] * row_scale).astype(BF16)
+
     actions = both(action_states, 1)
     depth = joined.shape[0]
 
@@ -176,6 +173,7 @@
         return cut(actions, row * depth, depth, 1)
 
     row_c, block_c = weight_last
+    later, block_c = lax.optimization_barrier((expert_out, block_c))
     blocks = [(mine, joined)]
     for row_a, block_a, row_b, block_b in weight_pairs:
         blocks += [(row_a, block_a), (row_b, block_b)]
@@ -196,7 +194,6 @@
     action_key = projected[:, query_cols : query_cols + key_cols]
     action_value = projected[:, query_cols + key_cols :]
 
-    later, _ = lax.optimization_barrier((expert_out, block_c))
     out_pairs, out_last = gather(later)
     piece = expert_out.shape[1]
     out_weight = jnp.zeros((expert_out.shape[0], piece * count), BF16)

time: 222 us -> 229 us (1.032)
  waiting for transfers between devices: 87.1 us -> 99.1 us
  starting transfers between devices: 47.5 us -> 39.4 us
  other arithmetic: 9.11 us -> 12.6 us
    ppermute x6, waiting for transfers between devices: 0.02 us -> 19.3 us  [gather(): back_block = lax.ppermute(back_block, 'row', back)]
    ppermute x2, waiting for transfers between devices: 17.6 us -> 12 us  [gather(): lax.ppermute(back_block[half:], 'row', back)]
    ppermute x6, starting transfers between devices: 16.7 us -> 11.7 us  [gather(): ahead_block = lax.ppermute(ahead_block, 'row', ahead)]
    ppermute x17 -> x7, starting transfers between devices: 24.3 us -> 21.7 us  [shards(): lax.ppermute(cut(outgoing, row_at(step) * own, own, 0), 'row', pairs)]
    ppermute x2, starting transfers between devices: 4.89 us -> 2.39 us  [gather(): lax.ppermute(ahead_block[:half], 'row', ahead)]
    ppermute x17 -> x7, waiting for transfers between devices: 60.2 us -> 61.7 us  [shards(): lax.ppermute(cut(outgoing, row_at(step) * own, own, 0), 'row', pairs)]
    unnamed x26 -> x36, local copies, waits for them, and re-layouts: 11.9 us -> 11.7 us
  transfers between devices with their start and end apart: 36 -> 26, of which waited for: 13 -> 9; matrix products, arithmetic and copies ran while one was open for 18% -> 22% of each run, Pallas kernels for 0% -> 9%
where the time goes in v4:
time: 229 us; the launch traced here: 228 us
  waiting for transfers between devices  99.1 us (43%)
  starting transfers between devices  39.4 us (17%)
  matrix products  27.7 us (12%)
  Pallas kernels  21.3 us (9%)
  local copies, waits for them, and re-layouts  17 us (7%)
  other arithmetic  12.6 us (6%)
  between operations  11.2 us (5%)
    ppermute x7, waiting for transfers between devices, shards(): lax.ppermute(cut(outgoing, row_at(step) * own, own, 0), 'row', pairs)  61.7 us
    ppermute x7, starting transfers between devices, shards(): lax.ppermute(cut(outgoing, row_at(step) * own, own, 0), 'row', pairs)  21.7 us
    pallas_call x1, Pallas kernels, attend(): pl.pallas_call(functools.partial(attend_kernel, HEAD ** (-0.5) * math.log...  21.3 us
    ppermute x6, waiting for transfers between devices, gather(): back_block = lax.ppermute(back_block, 'row', back)  19.3 us
    dot_general x2, matrix products, product_of(): jnp.dot(jnp.concatenate([columns(row) for row, _ in some], axis=1), jnp.c...  16.2 us
    ppermute x2, waiting for transfers between devices, gather(): lax.ppermute(back_block[half:], 'row', back)  12 us
    ppermute x6, starting transfers between devices, gather(): ahead_block = lax.ppermute(ahead_block, 'row', ahead)  11.7 us
    unnamed x36, local copies, waits for them, and re-layouts  11.7 us
  transfers between devices with their start and end apart: 26, of which 9 were waited for; matrix products, arithmetic and copies ran while one was open for 22% of the time, Pallas kernels for 9%

profile of v4, /device:TPU:0, one launch (start us, length us, event | category | flops | bytes accessed | tf_op | source)
XLA Modules:
  0.0 228.3 jit_solution(1248662375525562476)
XLA Ops:
  1.2 2.2 constant_dynamic-update-slice_fusion.9
  7.0 2.7 %collective-permute-start.8 = (bf16[256,2048]{1,0:T(8,128)(2,1)}, bf16[256,2048]{1,0:T(8,128)(2,1)}, u32[]{:S(2)}, u32[]{:S(2)}) collective-permute-start(bf16[256,2048]{1,0:T(8,128)(2,1)} %get-tuple-element.51), channel_id=1, source_target_pairs={{0,4},{4,8},{8,12},{12,14},{14,10},{10,6},{6,2},{2,0},{1,5},{5,9},... | collective-permute-start | bytes 3145736 | tf_op jit(solution)/shard_map/ppermute | solution.py:113
  18.8 2.6 %fusion.16 = f32[1024,512]{1,0:T(8,128)} fusion(bf16[1024,512]{1,0:T(8,128)(2,1)S(1)} %copy-done.13, bf16[1024,1024]{1,0:T(8,128)(2,1)S(1)} %pad_maximum_fusion, f32[1024]{0:T(1024)S(1)} %copy-done.14), kind=kOutput, calls=%fused_computation.38 | convolution fusion | flops 1076887552 | bytes 5246976 | tf_op jit(solution)/shard_map/dot_general | solution.py:139
  26.9 2.6 %collective-permute-start.2 = (bf16[128,1152]{1,0:T(8,128)(2,1)}, bf16[128,1152]{1,0:T(8,128)(2,1)}, u32[]{:S(2)}, u32[]{:S(2)}) collective-permute-start(bf16[128,1152]{1,0:T(8,128)(2,1)} %get-tuple-element.42), channel_id=1, source_target_pairs={{0,8},{4,12},{8,14},{12,10},{14,6},{10,2},{6,0},{2,4},{1,9},{5,13}... | collective-permute-start | bytes 884744 | tf_op jit(solution)/shard_map/ppermute | solution.py:152
  37.9 2.8 %collective-permute-start.3 = (bf16[128,1152]{1,0:T(8,128)(2,1)S(1)}, bf16[128,1152]{1,0:T(8,128)(2,1)S(1)}, u32[]{:S(2)}, u32[]{:S(2)}) collective-permute-start(bf16[128,1152]{1,0:T(8,128)(2,1)S(1)} %copy-done.12), channel_id=1, source_target_pairs={{0,12},{4,14},{8,10},{12,6},{14,2},{10,0},{6,4},{2,8},{1,13},{5,15... | collective-permute-start | bytes 884744 | tf_op jit(solution)/shard_map/ppermute | solution.py:152
  40.7 10.5 %collective-permute-start.4 = (bf16[128,1152]{1,0:T(8,128)(2,1)S(1)}, bf16[128,1152]{1,0:T(8,128)(2,1)S(1)}, u32[]{:S(2)}, u32[]{:S(2)}) collective-permute-start(bf16[128,1152]{1,0:T(8,128)(2,1)S(1)} %copy-done.11), channel_id=1, source_target_pairs={{0,14},{4,10},{8,6},{12,2},{14,0},{10,4},{6,8},{2,12},{1,15},{5,11... | collective-permute-start | bytes 884744 | tf_op jit(solution)/shard_map/ppermute | solution.py:152
  51.2 3.7 %collective-permute-start.5 = (bf16[128,1152]{1,0:T(8,128)(2,1)S(1)}, bf16[128,1152]{1,0:T(8,128)(2,1)S(1)}, u32[]{:S(2)}, u32[]{:S(2)}) collective-permute-start(bf16[128,1152]{1,0:T(8,128)(2,1)S(1)} %copy-done.10), channel_id=1, source_target_pairs={{0,10},{4,6},{8,2},{12,0},{14,4},{10,8},{6,12},{2,14},{1,11},{5,7}... | collective-permute-start | bytes 884744 | tf_op jit(solution)/shard_map/ppermute | solution.py:152
  55.3 47.7 %collective-permute-done.3 = bf16[128,1152]{1,0:T(8,128)(2,1)S(1)} collective-permute-done((bf16[128,1152]{1,0:T(8,128)(2,1)S(1)}, bf16[128,1152]{1,0:T(8,128)(2,1)S(1)}, u32[]{:S(2)}, u32[]{:S(2)}) %collective-permute-start.3) | collective-permute-done | bytes 294944 | tf_op jit(solution)/shard_map/ppermute | solution.py:152
  103.2 2.3 %constant_dynamic-update-slice_fusion.6 = bf16[1280,2048]{1,0:T(8,128)(2,1)} fusion(bf16[1280,2048]{1,0:T(8,128)(2,1)} %get-tuple-element.50, bf16[256,2048]{1,0:T(8,128)(2,1)} %collective-permute-done.8), kind=kLoop, calls=%fused_computation.73 | loop fusion | bytes 2097152
  105.5 2.3 %constant_dynamic-update-slice_fusion.5 = bf16[1280,2048]{1,0:T(8,128)(2,1)} fusion(bf16[1280,2048]{1,0:T(8,128)(2,1)} %constant_dynamic-update-slice_fusion.6, bf16[256,2048]{1,0:T(8,128)(2,1)} %collective-permute-done.10), kind=kLoop, calls=%fused_computation.72 | loop fusion | bytes 2097152
  107.8 8.8 %collective-permute-done.6 = bf16[128,1152]{1,0:T(8,128)(2,1)S(1)} collective-permute-done((bf16[128,1152]{1,0:T(8,128)(2,1)S(1)}, bf16[128,1152]{1,0:T(8,128)(2,1)S(1)}, u32[]{:S(2)}, u32[]{:S(2)}) %collective-permute-start.6) | collective-permute-done | bytes 294944 | tf_op jit(solution)/shard_map/ppermute | solution.py:152
  116.6 5.1 %collective-permute-done.7 = bf16[128,1152]{1,0:T(8,128)(2,1)S(1)} collective-permute-done((bf16[128,1152]{1,0:T(8,128)(2,1)S(1)}, bf16[128,1152]{1,0:T(8,128)(2,1)S(1)}, u32[]{:S(2)}, u32[]{:S(2)}) %collective-permute-start.7) | collective-permute-done | bytes 294944 | tf_op jit(solution)/shard_map/ppermute | solution.py:152
  121.8 2.0 collective-permute-start.13
  127.5 19.2 %collective-permute-done.14 = bf16[256,2048]{1,0:T(8,128)(2,1)S(1)} collective-permute-done((bf16[256,2048]{1,0:T(8,128)(2,1)S(1)}, bf16[256,2048]{1,0:T(8,128)(2,1)S(1)}, u32[]{:S(2)}, u32[]{:S(2)}) %collective-permute-start.14) | collective-permute-done | bytes 1048608 | tf_op jit(solution)/shard_map/ppermute | solution.py:114
  146.9 2.1 collective-permute-start.15
  151.9 8.0 %collective-permute-done.16 = bf16[128,2048]{1,0:T(8,128)(2,1)S(1)} collective-permute-done((bf16[128,2048]{1,0:T(8,128)(2,1)S(1)}, bf16[128,2048]{1,0:T(8,128)(2,1)S(1)}, u32[]{:S(2)}, u32[]{:S(2)}) %collective-permute-start.16) | collective-permute-done | bytes 524320 | tf_op jit(solution)/shard_map/ppermute | solution.py:120
  162.1 10.3 %fusion.45 = f32[1024,2048]{1,0:T(8,128)} fusion(bf16[1024,1280]{1,0:T(8,128)(2,1)S(1)} %fusion.35, bf16[1280,2048]{1,0:T(8,128)(2,1)} %constant_dynamic-update-slice_fusion.3), kind=kOutput, calls=%fused_computation.103 | convolution fusion | flops 5368709120 | bytes 16252928 | tf_op jit(solution)/shard_map/dot_general | solution.py:184
  174.4 5.9 %add_convert_fusion = bf16[1024,2048]{1,0:T(8,128)(2,1)S(1)} fusion(f32[1024,2048]{1,0:T(8,128)} %fusion.45, bf16[256,2048]{1,0:T(8,128)(2,1)S(1)} %pad_maximum_fusion.1, bf16[256,2048]{1,0:T(8,128)(2,1)S(1)} %collective-permute-done.14, bf16[256,2048]{1,0:T(8,128)(2,1)S(1)} %collective-permute-done.13, bf16[1024,256]{1,0:T(8,128)(2,1)S(1)} %get-tuple-element.34, ...), kind=kOutput, calls=%fused_computation | convolution fusion | flops 3239575552 | bytes 17301504 | tf_op jit(solution)/shard_map/dot_general | solution.py:184
  180.7 3.8 %collective-permute-done.19 = bf16[1024,256]{1,0:T(8,128)(2,1)S(1)} collective-permute-done((bf16[1024,256]{1,0:T(8,128)(2,1)S(1)}, bf16[1024,256]{1,0:T(8,128)(2,1)S(1)}, u32[]{:S(2)}, u32[]{:S(2)}) %collective-permute-start.19) | collective-permute-done | bytes 524320 | tf_op jit(solution)/shard_map/ppermute | solution.py:113
  186.5 21.3 %attend.1 = bf16[1024,1024]{1,0:T(8,128)(2,1)S(1)} custom-call(s32[1]{0:T(128)S(6)} %copy.46.plen_ref, s32[1]{0:T(128)S(6)} %copy.47.alen_ref, bf16[1024,1024]{1,0:T(8,128)(2,1)S(1)} %slice.87.q_ref, bf16[128,512]{1,0:T(8,128)(2,1)S(1)} %get-tuple-element.47.pk_ref, bf16[1024,512]{1,0:T(8,128)(2,1)S(1)} %get-tuple-element.30.ak_ref, ...), custom_call_target="tpu_custom_call" | custom-call | flops 9663676416 | bytes 4194304 | tf_op jit(solution)/shard_map/attend/pallas_call | solution.py:49
  210.4 4.0 %collective-permute-done.24 = bf16[512,256]{1,0:T(8,128)(2,1)S(1)} collective-permute-done((bf16[512,256]{1,0:T(8,128)(2,1)S(1)}, bf16[512,256]{1,0:T(8,128)(2,1)S(1)}, u32[]{:S(2)}, u32[]{:S(2)}) %collective-permute-start.24) | collective-permute-done | bytes 262176 | tf_op jit(solution)/shard_map/ppermute | solution.py:120
  216.4 3.7 %fusion.11 = bf16[1024,1024]{1,0:T(8,128)(2,1)} fusion(bf16[1024,1024]{1,0:T(8,128)(2,1)S(1)} %attend.1, bf16[1024,2048]{1,0:T(8,128)(2,1)S(1)} %maximum_dynamic-update-slice_fusion, u32[]{:T(128)S(6)} %mul.166), kind=kOutput, calls=%fused_computation.36 | convolution fusion | flops 2148532224 | bytes 6291460 | tf_op jit(solution)/shard_map/dot_general | solution.py:214
  220.0 4.0 %fusion.9 = f32[1024,1024]{1,0:T(8,128)S(1)} fusion(bf16[1024,1024]{1,0:T(8,128)(2,1)S(1)} %attend.1, bf16[1024,2048]{1,0:T(8,128)(2,1)} %copy-done.5, u32[]{:T(128)S(6)} %mul.165), kind=kOutput, calls=%fused_computation.32 | convolution fusion | flops 2147483648 | bytes 8388612 | tf_op jit(solution)/shard_map/dot_general | solution.py:214
  224.5 3.8 %add_convert_fusion.1 = bf16[1024,1024]{1,0:T(8,128)(2,1)} fusion(f32[1024,1024]{1,0:T(8,128)S(1)} %fusion.9, bf16[1024,1024]{1,0:T(8,128)(2,1)} %collective-permute-done.25), kind=kLoop, calls=%fused_computation.23 | loop fusion | flops 3145728 | bytes 8388608 | tf_op jit(solution)/shard_map/convert_element_type | solution.py:219
  (110 shorter events, 35.8 us)
Async XLA Ops:
  0.6 14.8 %collective-permute-start = (bf16[512,1024]{1,0:T(8,128)(2,1)}, bf16[512,1024]{1,0:T(8,128)(2,1)S(1)}, u32[]{:S(2)}, u32[]{:S(2)}) collective-permute-start(bf16[512,1024]{1,0:T(8,128)(2,1)} %param.12), channel_id=1, source_target_pairs={{0,1},{1,0},{2,3},{3,2},{4,5},{5,4},{6,7},{7,6},{8,9},{9,8},{10,11... | collective-permute-start | bytes 3145736 | tf_op jit(solution)/shard_map/ppermute | solution.py:127
  7.0 28.2 %collective-permute-start.8 = (bf16[256,2048]{1,0:T(8,128)(2,1)}, bf16[256,2048]{1,0:T(8,128)(2,1)}, u32[]{:S(2)}, u32[]{:S(2)}) collective-permute-start(bf16[256,2048]{1,0:T(8,128)(2,1)} %get-tuple-element.51), channel_id=1, source_target_pairs={{0,4},{4,8},{8,12},{12,14},{14,10},{10,6},{6,2},{2,0},{1,5},{5,9},... | collective-permute-start | bytes 3145736 | tf_op jit(solution)/shard_map/ppermute | solution.py:113
  9.7 27.1 %collective-permute-start.10 = (bf16[256,2048]{1,0:T(8,128)(2,1)}, bf16[256,2048]{1,0:T(8,128)(2,1)}, u32[]{:S(2)}, u32[]{:S(2)}) collective-permute-start(bf16[256,2048]{1,0:T(8,128)(2,1)} %get-tuple-element.51), channel_id=1, source_target_pairs={{4,0},{8,4},{12,8},{14,12},{10,14},{6,10},{2,6},{0,2},{5,1},{9,5},... | collective-permute-start | bytes 3145736 | tf_op jit(solution)/shard_map/ppermute | solution.py:114
  24.9 15.9 %collective-permute-start.1 = (bf16[128,1152]{1,0:T(8,128)(2,1)}, bf16[128,1152]{1,0:T(8,128)(2,1)}, u32[]{:S(2)}, u32[]{:S(2)}) collective-permute-start(bf16[128,1152]{1,0:T(8,128)(2,1)} %get-tuple-element.43), channel_id=1, source_target_pairs={{0,4},{4,8},{8,12},{12,14},{14,10},{10,6},{6,2},{2,0},{1,5},{5,9},... | collective-permute-start | bytes 884744 | tf_op jit(solution)/shard_map/ppermute | solution.py:152
  26.9 24.4 %collective-permute-start.2 = (bf16[128,1152]{1,0:T(8,128)(2,1)}, bf16[128,1152]{1,0:T(8,128)(2,1)}, u32[]{:S(2)}, u32[]{:S(2)}) collective-permute-start(bf16[128,1152]{1,0:T(8,128)(2,1)} %get-tuple-element.42), channel_id=1, source_target_pairs={{0,8},{4,12},{8,14},{12,10},{14,6},{10,2},{6,0},{2,4},{1,9},{5,13}... | collective-permute-start | bytes 884744 | tf_op jit(solution)/shard_map/ppermute | solution.py:152
  35.2 86.5 %collective-permute-start.9 = (bf16[256,2048]{1,0:T(8,128)(2,1)}, bf16[256,2048]{1,0:T(8,128)(2,1)S(1)}, u32[]{:S(2)}, u32[]{:S(2)}) collective-permute-start(bf16[256,2048]{1,0:T(8,128)(2,1)} %collective-permute-done.8), channel_id=1, source_target_pairs={{0,4},{4,8},{8,12},{12,14},{14,10},{10,6},{6,2},{2,0},{1,5},{5,9},... | collective-permute-start | bytes 3145736 | tf_op jit(solution)/shard_map/ppermute | solution.py:113
  36.8 85.0 %collective-permute-start.11 = (bf16[256,2048]{1,0:T(8,128)(2,1)}, bf16[256,2048]{1,0:T(8,128)(2,1)S(1)}, u32[]{:S(2)}, u32[]{:S(2)}) collective-permute-start(bf16[256,2048]{1,0:T(8,128)(2,1)} %collective-permute-done.10), channel_id=1, source_target_pairs={{4,0},{8,4},{12,8},{14,12},{10,14},{6,10},{2,6},{0,2},{5,1},{9,5},... | collective-permute-start | bytes 3145736 | tf_op jit(solution)/shard_map/ppermute | solution.py:114
  37.9 65.1 %collective-permute-start.3 = (bf16[128,1152]{1,0:T(8,128)(2,1)S(1)}, bf16[128,1152]{1,0:T(8,128)(2,1)S(1)}, u32[]{:S(2)}, u32[]{:S(2)}) collective-permute-start(bf16[128,1152]{1,0:T(8,128)(2,1)S(1)} %copy-done.12), channel_id=1, source_target_pairs={{0,12},{4,14},{8,10},{12,6},{14,2},{10,0},{6,4},{2,8},{1,13},{5,15... | collective-permute-start | bytes 884744 | tf_op jit(solution)/shard_map/ppermute | solution.py:152
  40.7 62.3 %collective-permute-start.4 = (bf16[128,1152]{1,0:T(8,128)(2,1)S(1)}, bf16[128,1152]{1,0:T(8,128)(2,1)S(1)}, u32[]{:S(2)}, u32[]{:S(2)}) collective-permute-start(bf16[128,1152]{1,0:T(8,128)(2,1)S(1)} %copy-done.11), channel_id=1, source_target_pairs={{0,14},{4,10},{8,6},{12,2},{14,0},{10,4},{6,8},{2,12},{1,15},{5,11... | collective-permute-start | bytes 884744 | tf_op jit(solution)/shard_map/ppermute | solution.py:152
  51.2 51.9 %collective-permute-start.5 = (bf16[128,1152]{1,0:T(8,128)(2,1)S(1)}, bf16[128,1152]{1,0:T(8,128)(2,1)S(1)}, u32[]{:S(2)}, u32[]{:S(2)}) collective-permute-start(bf16[128,1152]{1,0:T(8,128)(2,1)S(1)} %copy-done.10), channel_id=1, source_target_pairs={{0,10},{4,6},{8,2},{12,0},{14,4},{10,8},{6,12},{2,14},{1,11},{5,7}... | collective-permute-start | bytes 884744 | tf_op jit(solution)/shard_map/ppermute | solution.py:152
  103.0 13.6 %collective-permute-start.6 = (bf16[128,1152]{1,0:T(8,128)(2,1)S(1)}, bf16[128,1152]{1,0:T(8,128)(2,1)S(1)}, u32[]{:S(2)}, u32[]{:S(2)}) collective-permute-start(bf16[128,1152]{1,0:T(8,128)(2,1)S(1)} %copy-done.9), channel_id=1, source_target_pairs={{0,6},{4,2},{8,0},{12,4},{14,8},{10,12},{6,14},{2,10},{1,7},{5,3},... | collective-permute-start | bytes 884744 | tf_op jit(solution)/shard_map/ppermute | solution.py:152
  103.0 18.7 %collective-permute-start.7 = (bf16[128,1152]{1,0:T(8,128)(2,1)S(1)}, bf16[128,1152]{1,0:T(8,128)(2,1)S(1)}, u32[]{:S(2)}, u32[]{:S(2)}) collective-permute-start(bf16[128,1152]{1,0:T(8,128)(2,1)S(1)} %get-tuple-element.37), channel_id=1, source_target_pairs={{0,2},{4,0},{8,4},{12,8},{14,12},{10,14},{6,10},{2,6},{1,3},{5,1},... | collective-permute-start | bytes 884744 | tf_op jit(solution)/shard_map/ppermute | solution.py:152
  103.1 45.8 %collective-permute-start.12 = (bf16[1024,1024]{1,0:T(8,128)(2,1)S(1)}, bf16[1024,1024]{1,0:T(8,128)(2,1)S(1)}, u32[]{:S(2)}, u32[]{:S(2)}) collective-permute-start(bf16[1024,1024]{1,0:T(8,128)(2,1)S(1)} %copy-done.6), channel_id=1, source_target_pairs={{0,1},{1,0},{2,3},{3,2},{4,5},{5,4},{6,7},{7,6},{8,9},{9,8},{10,11... | collective-permute-start | bytes 6291464 | tf_op jit(solution)/shard_map/ppermute | solution.py:127
  121.7 25.0 %collective-permute-start.14 = (bf16[256,2048]{1,0:T(8,128)(2,1)S(1)}, bf16[256,2048]{1,0:T(8,128)(2,1)S(1)}, u32[]{:S(2)}, u32[]{:S(2)}) collective-permute-start(bf16[256,2048]{1,0:T(8,128)(2,1)S(1)} %collective-permute-done.11), channel_id=1, source_target_pairs={{4,0},{8,4},{12,8},{14,12},{10,14},{6,10},{2,6},{0,2},{5,1},{9,5},... | collective-permute-start | bytes 3145736 | tf_op jit(solution)/shard_map/ppermute | solution.py:114
  121.8 25.1 %collective-permute-start.13 = (bf16[256,2048]{1,0:T(8,128)(2,1)S(1)}, bf16[256,2048]{1,0:T(8,128)(2,1)S(1)}, u32[]{:S(2)}, u32[]{:S(2)}) collective-permute-start(bf16[256,2048]{1,0:T(8,128)(2,1)S(1)} %collective-permute-done.9), channel_id=1, source_target_pairs={{0,4},{4,8},{8,12},{12,14},{14,10},{10,6},{6,2},{2,0},{1,5},{5,9},... | collective-permute-start | bytes 3145736 | tf_op jit(solution)/shard_map/ppermute | solution.py:113
  146.8 13.1 %collective-permute-start.16 = (bf16[128,2048]{1,0:T(8,128)(2,1)S(1)}, bf16[128,2048]{1,0:T(8,128)(2,1)S(1)}, u32[]{:S(2)}, u32[]{:S(2)}) collective-permute-start(bf16[128,2048]{1,0:T(8,128)(2,1)S(1)} %slice.86), channel_id=1, source_target_pairs={{4,0},{8,4},{12,8},{14,12},{10,14},{6,10},{2,6},{0,2},{5,1},{9,5},... | collective-permute-start | bytes 1572872 | tf_op jit(solution)/shard_map/ppermute | solution.py:120
  146.9 13.0 %collective-permute-start.15 = (bf16[128,2048]{1,0:T(8,128)(2,1)S(1)}, bf16[128,2048]{1,0:T(8,128)(2,1)S(1)}, u32[]{:S(2)}, u32[]{:S(2)}) collective-permute-start(bf16[128,2048]{1,0:T(8,128)(2,1)S(1)} %slice.85), channel_id=1, source_target_pairs={{0,4},{4,8},{8,12},{12,14},{14,10},{10,6},{6,2},{2,0},{1,5},{5,9},... | collective-permute-start | bytes 1572872 | tf_op jit(solution)/shard_map/ppermute | solution.py:119
  160.0 12.3 %collective-permute-start.17 = (bf16[1024,256]{1,0:T(8,128)(2,1)S(1)}, bf16[1024,256]{1,0:T(8,128)(2,1)S(1)}, u32[]{:S(2)}, u32[]{:S(2)}) collective-permute-start(bf16[1024,256]{1,0:T(8,128)(2,1)S(1)} %copy-done.8), channel_id=1, source_target_pairs={{0,4},{4,8},{8,12},{12,14},{14,10},{10,6},{6,2},{2,0},{1,5},{5,9},... | collective-permute-start | bytes 1572872 | tf_op jit(solution)/shard_map/ppermute | solution.py:113
  161.9 12.3 %collective-permute-start.18 = (bf16[1024,256]{1,0:T(8,128)(2,1)S(1)}, bf16[1024,256]{1,0:T(8,128)(2,1)S(1)}, u32[]{:S(2)}, u32[]{:S(2)}) collective-permute-start(bf16[1024,256]{1,0:T(8,128)(2,1)S(1)} %copy-done.8), channel_id=1, source_target_pairs={{4,0},{8,4},{12,8},{14,12},{10,14},{6,10},{2,6},{0,2},{5,1},{9,5},... | collective-permute-start | bytes 1572872 | tf_op jit(solution)/shard_map/ppermute | solution.py:114
  172.4 12.1 %collective-permute-start.19 = (bf16[1024,256]{1,0:T(8,128)(2,1)S(1)}, bf16[1024,256]{1,0:T(8,128)(2,1)S(1)}, u32[]{:S(2)}, u32[]{:S(2)}) collective-permute-start(bf16[1024,256]{1,0:T(8,128)(2,1)S(1)} %collective-permute-done.17), channel_id=1, source_target_pairs={{0,4},{4,8},{8,12},{12,14},{14,10},{10,6},{6,2},{2,0},{1,5},{5,9},... | collective-permute-start | bytes 1572872 | tf_op jit(solution)/shard_map/ppermute | solution.py:113
  174.2 12.1 %collective-permute-start.20 = (bf16[1024,256]{1,0:T(8,128)(2,1)S(1)}, bf16[1024,256]{1,0:T(8,128)(2,1)S(1)}, u32[]{:S(2)}, u32[]{:S(2)}) collective-permute-start(bf16[1024,256]{1,0:T(8,128)(2,1)S(1)} %collective-permute-done.18), channel_id=1, source_target_pairs={{4,0},{8,4},{12,8},{14,12},{10,14},{6,10},{2,6},{0,2},{5,1},{9,5},... | collective-permute-start | bytes 1572872 | tf_op jit(solution)/shard_map/ppermute | solution.py:114
  184.5 25.4 %collective-permute-start.21 = (bf16[1024,256]{1,0:T(8,128)(2,1)S(1)}, bf16[1024,256]{1,0:T(8,128)(2,1)S(1)}, u32[]{:S(2)}, u32[]{:S(2)}) collective-permute-start(bf16[1024,256]{1,0:T(8,128)(2,1)S(1)} %collective-permute-done.19), channel_id=1, source_target_pairs={{0,4},{4,8},{8,12},{12,14},{14,10},{10,6},{6,2},{2,0},{1,5},{5,9},... | collective-permute-start | bytes 1572872 | tf_op jit(solution)/shard_map/ppermute | solution.py:113
  186.3 21.7 %collective-permute-start.22 = (bf16[1024,256]{1,0:T(8,128)(2,1)S(1)}, bf16[1024,256]{1,0:T(8,128)(2,1)S(1)}, u32[]{:S(2)}, u32[]{:S(2)}) collective-permute-start(bf16[1024,256]{1,0:T(8,128)(2,1)S(1)} %collective-permute-done.20), channel_id=1, source_target_pairs={{4,0},{8,4},{12,8},{14,12},{10,14},{6,10},{2,6},{0,2},{5,1},{9,5},... | collective-permute-start | bytes 1572872 | tf_op jit(solution)/shard_map/ppermute | solution.py:114
  209.9 6.4 %collective-permute-start.23 = (bf16[512,256]{1,0:T(8,128)(2,1)S(1)}, bf16[512,256]{1,0:T(8,128)(2,1)S(1)}, u32[]{:S(2)}, u32[]{:S(2)}) collective-permute-start(bf16[512,256]{1,0:T(8,128)(2,1)S(1)} %slice.90), channel_id=1, source_target_pairs={{0,4},{4,8},{8,12},{12,14},{14,10},{10,6},{6,2},{2,0},{1,5},{5,9},... | collective-permute-start | bytes 786440 | tf_op jit(solution)/shard_map/ppermute | solution.py:119
  (17 other events, 334.6 us)
